TPU v7x, 32 devices: a whole 2x2x4 slice. The times are simulated.
32 devices in a mesh: fsdp: 4 (over z), context: 4 (over y, x), tensor: 2 (over core).
Axes of the slice: x: 2, y: 2, z: 4, core: 2. Of those that a mesh axis runs over, the one named last changes fastest.
Arguments:
- tokens_in: bfloat16 [4096, 768], P(('fsdp', 'context')), may hold values from -6 to 6
- chars_in: bfloat16 [6144, 768], P(('fsdp', 'context')), may hold values from -6 to 6
- segment_ids: int32 [4, 1024], P('fsdp'), may hold values from 0 to 3, never falling along the last dimension, each value on 1 to 512 neighbouring positions
- char_counts: int32 [16, 256], P(('fsdp', 'context')), may hold values from 1 to 4, 384 in all within a row
- valid: int32 [4, 1024], P('fsdp', 'context'), may hold values 0 or 1
- teacher_tokens: bfloat16 [4096, 768], P(('fsdp', 'context')), may hold values from -6 to 6
- teacher_chars: bfloat16 [6144, 768], P(('fsdp', 'context')), may hold values from -6 to 6
- w_qkv: bfloat16 [1, 768, 3, 768], P(None, 'fsdp', None, 'tensor'), may hold values from -0.21875 to 0.21875
- w_out: bfloat16 [1, 768, 768], P(None, 'tensor', 'fsdp'), may hold values from -0.3125 to 0.3125
- w_up: bfloat16 [1, 768, 3072], P(None, 'fsdp', 'tensor'), may hold values from -0.21875 to 0.21875
- w_down: bfloat16 [1, 3072, 768], P(None, 'tensor', 'fsdp'), may hold values from -0.15625 to 0.15625
- w_gru: bfloat16 [1, 768, 4, 384], P(None, 'fsdp', None, 'tensor'), may hold values from -0.21875 to 0.21875
- gru_bias: float32 [1, 2, 384], P(None, None, 'tensor'), may hold values from -7 to 0
- w_tok: bfloat16 [1, 768, 768], P(None, 'fsdp', 'tensor'), may hold values from -0.21875 to 0.21875
- w_char: bfloat16 [1, 2, 384, 768], P(None, None, 'tensor', 'fsdp'), may hold values from -0.625 to 0.625
- w_conv: bfloat16 [1, 3, 2, 768, 1536], P(None, None, None, 'tensor', 'fsdp'), may hold values from -0.09375 to 0.09375
- ln_gain: float32 [1, 4, 768], replicated, may hold values from 0.5 to 1.5
- ln_bias: float32 [1, 4, 768], replicated, may hold values from -2 to 2
Outputs:
- token_out: float32 [4096, 768], P(('fsdp', 'context'))
- char_out: float32 [6144, 768], P(('fsdp', 'context'))
- loss: float32 [], replicated
- grad_tokens: float32 [4096, 768], P(('fsdp', 'context'))
- grad_chars: float32 [6144, 768], P(('fsdp', 'context'))
- grad_qkv: float32 [1, 768, 3, 768], P(None, 'fsdp', None, 'tensor')
- grad_out: float32 [1, 768, 768], P(None, 'tensor', 'fsdp')
- grad_up: float32 [1, 768, 3072], P(None, 'fsdp', 'tensor')
- grad_down: float32 [1, 3072, 768], P(None, 'tensor', 'fsdp')
- grad_gru: float32 [1, 768, 4, 384], P(None, 'fsdp', None, 'tensor')
- grad_gru_bias: float32 [1, 2, 384], P(None, None, 'tensor')
- grad_tok: float32 [1, 768, 768], P(None, 'fsdp', 'tensor')
- grad_char: float32 [1, 2, 384, 768], P(None, None, 'tensor', 'fsdp')
- grad_conv: float32 [1, 3, 2, 768, 1536], P(None, None, None, 'tensor', 'fsdp')
- grad_gain: float32 [1, 4, 768], replicated
- grad_shift: float32 [1, 4, 768], replicated
Inputs may be any that keep to these rules, and one draw needn't show every extreme that they name: `segment_ids`: in each sequence the ids never fall; each of the 4 documents covers one run of positions, at most 512 long, and one run has exactly 512. `char_counts`: each row sums to 384; its largest entry is exactly 4.
All inputs are finite; a program needn't handle non-finite values. No bound on the sum of `valid` on one device may be relied on, other than what follows from the above.
Results may differ from a plain program's by a relative error of at most 0.019.
Values may be sent and summed in bfloat16 or wider, within the bound.
No kernel may reach another device: no remote copies, remote signals or barrier semaphores. Data moves between devices by JAX's collectives and lax.ppermute only.
A program may use at most 192 MiB of HBM per device.

v0:
```python
import functools

import jax
import jax.numpy as jnp
from jax import lax
from jax.experimental import pallas as pl
from jax.experimental.pallas import tpu as pltpu
from jax.sharding import PartitionSpec as P

HD = 64
EPSILON = 1e-05
MASKED_SCORE = -1000000000.0
BF = jnp.bfloat16
F32 = jnp.float32
Z = "fsdp"
C = "context"
T = "tensor"
ROOM = 56 * 1024 * 1024


def dot(a, b, ca=1, cb=0):
    return lax.dot_general(a, b, (((ca,), (cb,)), ((), ())), preferred_element_type=F32)


def swap(x, axis, bit):
    size = lax.axis_size(axis)
    return lax.ppermute(x, axis, [(i, i ^ bit) for i in range(size)])


def turn(x, axis, k):
    size = lax.axis_size(axis)
    return lax.ppermute(x, axis, [(i, (i + k) % size) for i in range(size)])


def core_sum(x):
    return x + swap(x, T, 1)


def own_part(x, count, index, dim=0):
    width = x.shape[dim] // count
    return lax.dynamic_slice_in_dim(x, index * width, width, axis=dim)


def ordered(mine, other, first):
    return jnp.where(first, mine, other), jnp.where(first, other, mine)


def core_join(x, dim):
    other = swap(x, T, 1)
    low, high = ordered(x, other, lax.axis_index(T) == 0)
    return jnp.concatenate([low, high], axis=dim)


def after(x, *deps):
    return lax.optimization_barrier((x, deps))[0]


def whole(shape, dtype):
    return jax.ShapeDtypeStruct(shape, dtype)


def call(kernel, outs, name, scratch=()):
    return pl.pallas_call(
        kernel,
        out_shape=outs,
        scratch_shapes=list(scratch),
        compiler_params=pltpu.CompilerParams(vmem_limit_bytes=ROOM),
        cost_estimate=pl.CostEstimate(flops=1, bytes_accessed=1, transcendentals=0),
        name=name,
    )


def context_quarter(shard):
    return own_part(shard, 4, lax.axis_index(C))


def first_round(stack, wait_for):
    nz, _, n = stack.shape
    z = lax.axis_index(Z)
    half = n // 256 * 128
    index = [lax.rem(z + k, nz) for k in range(1, nz)]
    others = jnp.concatenate([lax.dynamic_slice_in_dim(stack, i, 1) for i in index])
    firsts = [after(others[:, :, cut], *wait_for) for cut in (slice(half), slice(half, n))]
    return firsts, [swap(a, C, b0) for a, (b0, _) in zip(firsts, BOTH)]


def second_round(firsts, nears, wait_for=()):
    both = [jnp.concatenate([a, b]) for a, b in zip(firsts, nears)]
    return [swap(after(x, *wait_for), C, b1) for x, (_, b1) in zip(both, BOTH)]


def assemble(shard, quads, widths):
    count, q = quads[0][0].shape[:2]
    nz = count + 1
    starts = [sum(widths[:i]) for i in range(len(widths))]

    def kernel(*refs):
        outs = refs[7:]
        z = lax.axis_index(Z)
        c = lax.axis_index(C)
        own = pl.ds(pl.multiple_of(z * 4 * q, 16), 4 * q)
        for out, begin, size in zip(outs, starts, widths):
            out[own] = refs[6][:, begin : begin + size]
        col = 0
        for side, (b0, b1) in enumerate(BOTH):
            first, near, far = refs[3 * side : 3 * side + 3]
            width = first.shape[-1]
            spans = []
            for out, begin, size in zip(outs, starts, widths):
                low, high = max(begin, col), min(begin + size, col + width)
                if low < high:
                    spans.append((out, slice(low - col, high - col), slice(low - begin, high - begin)))
            for ref, base, mask in ((first, 0, 0), (near, 0, b0), (far, 0, b1), (far, count, b0 ^ b1)):
                for s in range(count):
                    block = lax.rem(z + 1 + s, nz) * 4 + jnp.bitwise_xor(c, mask)
                    row = pl.multiple_of(block * q, 16)
                    for out, src, dst in spans:
                        out[pl.ds(row, q), dst] = ref[base + s, :, src]
            col += width

    shapes = tuple(whole((nz * 4 * q, w), BF) for w in widths)
    return call(kernel, shapes, "assemble")(*[x for quad in quads for x in quad], shard)


BOTH = ((1, 2), (2, 1))


def sent_apart(products, b0, b1):
    rows, width = products[0][0].shape[1], products[0][1].shape[1]
    arrays = []
    places = []
    for pair in products:
        spots = []
        for x in pair:
            for i, y in enumerate(arrays):
                if y is x:
                    break
            else:
                i = len(arrays)
                arrays.append(x)
            spots.append(i)
        places.append(spots)
    count = len(arrays)

    def kernel(*refs):
        outs = refs[count:]
        c = lax.axis_index(C)
        for j, (l, r) in enumerate(places):
            part = dot(refs[l][...], refs[r][...], 0, 0).astype(BF)
            if b1 is None:
                for m in range(4):

                    @pl.when(jnp.bitwise_xor(c, j) == m)
                    def _():
                        outs[m][...] = part
            else:
                slot = (j & b1) // b1
                mine = jnp.bitwise_and(jnp.bitwise_xor(c, j), b0) == 0

                @pl.when(mine)
                def _():
                    outs[0][slot] = part

                @pl.when(jnp.logical_not(mine))
                def _():
                    outs[1][slot] = part

    if b1 is None:
        shapes = (whole((rows, width), BF),) * 4
    else:
        shapes = (whole((2, rows, width), BF),) * 2
    return call(kernel, shapes, "grads")(*arrays)


def z_split(parts):
    nz = lax.axis_size(Z)
    rows, width = parts[0].shape
    block = rows // nz

    def kernel(*refs):
        z = lax.axis_index(Z)
        for k, out in enumerate(refs[len(parts) :]):
            at = pl.ds(pl.multiple_of(lax.rem(z + k, nz) * block, 16), block)
            total = refs[0][at].astype(F32)
            for ref in refs[1 : len(parts)]:
                total = total + ref[at].astype(F32)
            out[...] = total.astype(BF)

    return call(kernel, (whole((block, width), BF),) * nz, "z_split")(*parts)


def exchange(copied, split, wait_for=()):
    c = lax.axis_index(C)
    half = after(own_part(copied, 2, lax.axis_index(T), 1), *wait_for)
    pieces = [own_part(split, 4, jnp.bitwise_xor(c, m), 1) for m in range(4)]
    if half.shape[1] != pieces[0].shape[1]:
        return pieces[0], [(swap(half, C, m), swap(pieces[m], C, m)) for m in (1, 2, 3)]
    return pieces[0], [swap(jnp.concatenate([half, pieces[m]]), C, m) for m in (1, 2, 3)]


def collected(copied, own, came):
    rows = copied.shape[0]
    came = [x if isinstance(x, tuple) else (x[:rows], x[rows:]) for x in came]
    halves = jnp.concatenate([a for a, _ in came])
    return jnp.concatenate([copied, core_join(halves, 1)]), jnp.concatenate([own] + [b for _, b in came])


def by_context(parts, outs, stores, name):
    def kernel(*refs):
        c = lax.axis_index(C)
        for m in range(4):
            for j, store in enumerate(stores):

                @pl.when(jnp.bitwise_xor(c, m) == j)
                def _():
                    store(refs[m][...].astype(F32), refs[4:])

    return call(kernel, outs, name)(*parts)


def early_join(copies):
    _, rows, width = copies.shape
    third = width // 3

    def run(in_ref, up_ref, down_ref, tok_ref, char_ref, gru_ref):
        for j in range(4):
            at = slice(j * third, (j + 1) * third)
            up_ref[:, at] = in_ref[j, :, :third].astype(F32)
            down_ref[at] = in_ref[j, :, third : 2 * third].astype(F32).T
        tok_ref[...] = in_ref[0, :, 2 * third :].astype(F32)
        char_ref[...] = in_ref[1, :, 2 * third :].astype(F32).T
        gru_ref[:, :third] = in_ref[2, :, 2 * third :].astype(F32)
        gru_ref[:, third:] = in_ref[3, :, 2 * third :].astype(F32)

    shapes = (
        whole((rows, 4 * third), F32), whole((4 * third, rows), F32), whole((rows, third), F32),
        whole((third, rows), F32), whole((rows, 2 * third), F32),
    )
    return call(run, shapes, "early_join")(copies)


def query_join(parts):
    rows, width = parts[0].shape

    def put_out(x, outs):
        outs[0][...] = x.T

    def store(i):
        def put(x, outs):
            outs[1][:, i] = x

        return put

    outs = (whole((width, rows), F32), whole((rows, 3, width), F32))
    return by_context(parts, outs, (put_out, store(0), store(1), store(2)), "query_join")


def turned(blocks):
    return [turn(blocks[k], Z, k) for k in range(1, len(blocks))]


def summed(own, came):
    total = own.astype(F32)
    for x in came:
        total = total + x.astype(F32)
    return total.astype(BF)


def turned_all(x):
    return [x] + [turn(x, Z, k) for k in range(1, lax.axis_size(Z))]


def swapped(x):
    return [swap(x, C, m) for m in (1, 2, 3)]


BESIDE = 1 << 20


def gather_beside(x, dim):
    nz = lax.axis_size(Z)
    extent = x.shape[dim]
    other = x.size // extent
    unit = 128 if dim else 16
    need = -(-BESIDE // (2 * nz * other * unit)) * unit
    if need > extent:
        pads = [(0, 0)] * x.ndim
        pads[dim] = (0, need - extent)
        x = jnp.pad(x, pads)
    return lax.all_gather(x, Z)


def from_neighbours(first, last):
    c = lax.axis_index(C)
    size = lax.axis_size(C)
    both = jnp.stack([first, last])
    near, far = swap(both, C, 1), swap(both, C, 3)
    odd = jnp.bitwise_and(c, 1) == 1
    before = jnp.where(odd, near[1], far[1])
    beyond = jnp.where(odd, far[0], near[0])
    return jnp.where(c > 0, before, 0), jnp.where(c < size - 1, beyond, 0)


def shifted(x, by):
    rows = x.shape[0]
    at = lax.broadcasted_iota(jnp.int32, x.shape, 0)
    if by > 0:
        return jnp.where(at >= by, pltpu.roll(x, by, 0), 0.0)
    return jnp.where(at < rows + by, pltpu.roll(x, rows + by, 0), 0.0)


def block_of(k, nz):
    return lax.rem(lax.axis_index(Z) - k + nz, nz)


def conv_main(toks, chrs, kernel):
    nz = len(toks)
    half = toks[0].shape[1]
    rows = toks[0].shape[0] - 16
    cols = kernel.shape[-1]
    part = rows // 2

    def run(*refs):
        c_ref, w_ref, keep_ref, send_ref = refs[nz:]
        t = lax.axis_index(T)
        at = lax.broadcasted_iota(jnp.int32, (rows, cols), 0)
        for k in range(nz):
            j = block_of(k, nz)
            u = jnp.concatenate([refs[k][:rows], c_ref[j, :rows]], axis=1)
            rim = refs[k][rows:]
            rim = jnp.concatenate([rim[:2], rim[2:4]], axis=1)
            rim = jnp.concatenate([rim, jnp.zeros((14, 2 * half), BF)])
            total = dot(u, w_ref[1])
            total = total + jnp.where(at == 0, dot(rim, w_ref[0])[0:1], pltpu.roll(dot(u, w_ref[0]), 1, 0))
            total = total + jnp.where(at == rows - 1, dot(rim, w_ref[2])[1:2], pltpu.roll(dot(u, w_ref[2]), rows - 1, 0))

            @pl.when(t == 0)
            def _():
                keep_ref[k] = total[:part]
                send_ref[k] = total[part:]

            @pl.when(t != 0)
            def _():
                keep_ref[k] = total[part:]
                send_ref[k] = total[:part]

    shape = whole((nz, part, cols), F32)
    return call(run, (shape, shape), "conv")(*toks, chrs, kernel)


def add_split(keep, came):
    nz = keep.shape[0]

    def run(*refs):
        for k in range(nz):
            refs[2 + k][...] = (refs[0][k] + refs[1][k]).astype(BF)

    return call(run, (whole(keep.shape[1:], BF),) * nz, "add_split")(keep, came)


def side_by_side(parts, forward):
    nz = len(parts)
    rows, cols = parts[0].shape
    z = lax.axis_index(Z)
    if cols % 128:
        stacked = jnp.stack(parts)
        order = [lax.rem((s - z if forward else z - s) + nz, nz) for s in range(nz)]
        return jnp.concatenate([lax.dynamic_index_in_dim(stacked, i, 0, keepdims=False) for i in order], axis=1)

    def run(*refs):
        z = lax.axis_index(Z)
        for k in range(nz):
            s = lax.rem((z + k if forward else z - k + nz), nz)
            refs[nz][:, pl.ds(pl.multiple_of(s * cols, 128), cols)] = refs[k][...]

    return call(run, whole((rows, nz * cols), BF), "side_by_side")(*parts)


def column_slices(x, nz):
    cols = x.shape[1] // nz
    z = lax.axis_index(Z)
    return [lax.dynamic_slice_in_dim(x, lax.rem(z + k, nz) * cols, cols, axis=1) for k in range(nz)]


def row_norm(v):
    average = jnp.mean(v, axis=-1, keepdims=True)
    centered = v - average
    spread = jnp.mean(centered * centered, axis=-1, keepdims=True)
    inverse = lax.rsqrt(spread + EPSILON)
    return centered * inverse, inverse


def row_norm_back(e, n, inverse, gain):
    ge = e * gain
    one = jnp.mean(ge, axis=-1, keepdims=True)
    two = jnp.mean(ge * n, axis=-1, keepdims=True)
    return inverse * (ge - one - n * two)


def column_sum(x):
    return jnp.sum(x, axis=0, keepdims=True)


def close(second, y_mine, y_other, chars_in, teacher_tok, teacher_chr, pick, notes, marks, gains, shifts):
    rows, width = second.shape
    chars = chars_in.shape[0]
    half = rows // 2
    step = 128

    def run(
        s_ref, ym_ref, yo_ref, c_ref, tt_ref, tc_ref, pick_ref, vt_ref, vc_ref, g_ref, b_ref,
        tok_ref, chr_ref, d3_ref, d4_ref, dy_ref, stat_ref, y_ref, hi_ref, lo_ref,
    ):
        t = lax.axis_index(T)
        y_ref[pl.ds(pl.multiple_of(t * half, 16), half)] = ym_ref[...]
        y_ref[pl.ds(pl.multiple_of((1 - t) * half, 16), half)] = yo_ref[...]
        zero = jnp.zeros((1, width), F32)
        gain_sum, shift_sum, loss = zero, zero, zero
        for i in range(0, rows, step):
            at = slice(i, i + step)
            n, inverse = row_norm(s_ref[at] + y_ref[at, :width].astype(F32))
            out = n * g_ref[2:3] + b_ref[2:3]
            tok_ref[at] = out
            diff = out - tt_ref[at].astype(F32)
            e = vt_ref[at, 1:2] * diff
            loss += column_sum(e * diff)
            gain_sum += column_sum(e * n)
            shift_sum += column_sum(e)
            d3_ref[at] = row_norm_back(e, n, inverse, g_ref[2:3])
        stat_ref[0:1] = gain_sum
        stat_ref[2:3] = shift_sum
        gain_sum, shift_sum = zero, zero
        for i in range(0, chars, step):
            at = slice(i, i + step)
            spread = dot(pick_ref[:, at], y_ref[:, width:], 0, 0)
            n, inverse = row_norm(c_ref[at].astype(F32) + spread)
            out = n * g_ref[3:4] + b_ref[3:4]
            chr_ref[at] = out
            diff = out - tc_ref[at].astype(F32)
            e = vc_ref[at, 2:3] * diff
            loss += column_sum(e * diff)
            gain_sum += column_sum(e * n)
            shift_sum += column_sum(e)
            d = row_norm_back(e, n, inverse, g_ref[3:4])
            d4_ref[at] = d
            high = d.astype(BF)
            hi_ref[at] = high
            lo_ref[at] = (d - high.astype(F32)).astype(BF)
        stat_ref[1:2] = gain_sum
        stat_ref[3:4] = shift_sum
        stat_ref[4:5] = 0.5 * loss
        stat_ref[5:8] = jnp.zeros((3, width), F32)
        mine = pl.ds(pl.multiple_of(t * half, 16), half)
        own = pick_ref[mine]
        dy_ref[:, :width] = d3_ref[mine].astype(BF)
        dy_ref[:, width:] = (dot(own, hi_ref[...]) + dot(own, lo_ref[...])).astype(BF)

    return call(
        run,
        (
            whole((rows, width), F32), whole((chars, width), F32), whole((rows, width), F32),
            whole((chars, width), F32), whole((half, 2 * width), BF), whole((8, width), F32),
        ),
        "close",
        (pltpu.VMEM((rows, 2 * width), BF), pltpu.VMEM((chars, width), BF), pltpu.VMEM((chars, width), BF)),
    )(second, y_mine, y_other, chars_in, teacher_tok, teacher_chr, pick, notes, marks, gains, shifts)


def spread_taps(mine_ref, other_ref, wide, whole_ref):
    nz, part, cols = mine_ref.shape
    part -= 16
    rows = 2 * part
    t = lax.axis_index(T)
    at = lax.broadcasted_iota(jnp.int32, (rows, cols), 0)
    for k in range(nz):
        whole_ref[pl.ds(pl.multiple_of(t * part, 16), part)] = mine_ref[k, :part]
        whole_ref[pl.ds(pl.multiple_of((1 - t) * part, 16), part)] = other_ref[k, :part]
        a = mine_ref[k, part:].astype(F32)[0:1]
        b = other_ref[k, part:].astype(F32)[0:1]
        above, below = jnp.where(t == 0, a, b), jnp.where(t == 0, b, a)
        d = whole_ref[...].astype(F32)
        wide[1, k] = whole_ref[...]
        wide[0, k] = jnp.where(at == rows - 1, above, pltpu.roll(d, rows - 1, 0)).astype(BF)
        wide[2, k] = jnp.where(at == 0, below, pltpu.roll(d, 1, 0)).astype(BF)


def tap_scratch(mine):
    nz, part, cols = mine.shape
    rows = 2 * (part - 16)
    return pltpu.VMEM((3, nz, rows, cols), BF), pltpu.VMEM((rows, cols), BF)


def conv_back(mine, other, kernel):
    nz, part, cols = mine.shape
    rows = 2 * (part - 16)
    half = kernel.shape[1] // 2

    def run(*refs):
        m_ref, o_ref, w_ref = refs[:3]
        outs, (wide, whole_ref) = refs[3 : 3 + 2 * nz], refs[3 + 2 * nz :]
        spread_taps(m_ref, o_ref, wide, whole_ref)
        for k in range(nz):
            for side in range(2):
                at = slice(side * half, (side + 1) * half)
                x = sum(dot(wide[m, k], w_ref[m, at], 1, 1) for m in range(3)).astype(BF)
                if side:
                    outs[nz + k][...] = x
                else:
                    outs[k][...] = x

    shapes = (whole((rows, half), BF),) * (2 * nz)
    outs = call(run, shapes, "conv_back", tap_scratch(mine))(mine, other, kernel)
    return outs[:nz], outs[nz:]


def conv_grads(toks, chrs, mine, other):
    nz, part, cols = mine.shape
    rows = 2 * (part - 16)
    half = toks[0].shape[1]

    def run(*refs):
        c_ref, m_ref, o_ref, out_ref, wide, whole_ref = refs[nz:]
        spread_taps(m_ref, o_ref, wide, whole_ref)
        for m in range(3):
            for side in range(2):
                total = jnp.zeros((half, cols), F32)
                for k in range(nz):
                    u = c_ref[block_of(k, nz), :rows] if side else refs[k][:rows]
                    total += dot(u, wide[m, k], 0, 0)
                for r in range(2):
                    out_ref[2 * side + r, m] = total[r * half // 2 : (r + 1) * half // 2].astype(BF)

    shape = whole((4, 3, half // 2, cols), BF)
    return call(run, shape, "conv_grads", tap_scratch(mine))(*toks, chrs, mine, other)


def scan_pair(a, b, e, f):
    n = a.shape[0]
    rows = lax.broadcasted_iota(jnp.int32, a.shape, 0)
    step = 1
    while step < n:
        has = rows >= step
        pa = jnp.where(has, pltpu.roll(a, step, 0), 1.0)
        pb = jnp.where(has, pltpu.roll(b, step, 0), 0.0)
        b = b + a * pb
        a = a * pa
        has = rows < n - step
        pe = jnp.where(has, pltpu.roll(e, n - step, 0), 1.0)
        pf = jnp.where(has, pltpu.roll(f, n - step, 0), 0.0)
        f = f + e * pf
        e = e * pe
        step *= 2
    return a, b, e, f


def store_scans(scans, refs):
    a, b, e, f = scans
    n = a.shape[0]
    for ref, x in zip(refs[:4], scans):
        ref[...] = x
    ends = refs[4]
    ends[...] = jnp.zeros(ends.shape, F32)
    ends[0:1], ends[1:2], ends[2:3], ends[3:4] = a[n - 1 :], b[n - 1 :], e[:1], f[:1]


def scan_shapes(chars, units):
    return (whole((chars, units), F32),) * 4 + (whole((8, units), F32),)


def entering(refs):
    c = lax.axis_index(C)
    up = jnp.zeros((1, refs[0].shape[1]), F32)
    down = up
    for j in range(4):
        for m, ref in enumerate(refs):
            now = jnp.bitwise_xor(c, j) == m
            up = jnp.where(jnp.logical_and(now, j < c), ref[0:1] * up + ref[1:2], up)
    for j in (3, 2, 1, 0):
        for m, ref in enumerate(refs):
            now = jnp.bitwise_xor(c, j) == m
            down = jnp.where(jnp.logical_and(now, j > c), ref[2:3] * down + ref[3:4], down)
    return up, down


def gates(proj_ref, bias_ref, units):
    up = jax.nn.sigmoid(proj_ref[:, :units] + bias_ref[0:1])
    down = jax.nn.sigmoid(proj_ref[:, 2 * units : 3 * units] + bias_ref[1:2])
    return up, down


def gru_open(chars_in, w_recur, bias, marks):
    chars = chars_in.shape[0]
    units = bias.shape[1]

    def run(c_ref, w_ref, b_ref, m_ref, proj_ref, *outs):
        proj_ref[...] = dot(c_ref[...], w_ref[...])
        up, down = gates(proj_ref, b_ref, units)
        store_scans(
            scan_pair(
                (1.0 - up) * m_ref[:, 0:1], up * proj_ref[:, units : 2 * units],
                (1.0 - down) * m_ref[:, 1:2], down * proj_ref[:, 3 * units :],
            ),
            outs,
        )

    return call(run, (whole((chars, 4 * units), F32),) + scan_shapes(chars, units), "gru_open")(
        chars_in, w_recur, bias, marks
    )


def gru_close(scans, ends, pick, notes, w_charp_t):
    chars, units = scans[0].shape
    rows = pick.shape[0]
    half = w_charp_t.shape[0] // 2

    def run(cu, hu, cd, hd, e0, e1, e2, e3, p_ref, n_ref, w_ref, up_ref, down_ref, in_ref, pool_ref, keep_ref, send_ref):
        up, down = entering((e0, e1, e2, e3))
        in_ref[...] = jnp.zeros(in_ref.shape, F32)
        in_ref[0:1], in_ref[1:2] = up, down
        up_ref[...] = hu[...] + cu[...] * up
        down_ref[...] = hd[...] + cd[...] * down
        for ref, at in ((up_ref, slice(units)), (down_ref, slice(units, 2 * units))):
            pool_ref[:, at] = (dot(p_ref[...], ref[...].astype(BF)) / n_ref[:, 0:1]).astype(BF)
        t = lax.axis_index(T)
        low = dot(pool_ref[...], w_ref[:half], 1, 1)
        high = dot(pool_ref[...], w_ref[half:], 1, 1)
        keep_ref[...] = jnp.where(t == 0, low, high)
        send_ref[...] = jnp.where(t == 0, high, low)

    state = whole((chars, units), F32)
    return call(
        run,
        (
            state, state, whole((8, units), F32), whole((rows, 2 * units), BF),
            whole((rows, half), F32), whole((rows, half), F32),
        ),
        "gru_close",
    )(*scans, *ends, pick, notes, w_charp_t)


def gru_back_open(dfb, proj, bias, marks, pick, notes, w_charp_t):
    chars = proj.shape[0]
    units = bias.shape[1]

    def run(d_ref, proj_ref, b_ref, m_ref, p_ref, n_ref, w_ref, dh_ref, *outs):
        pooled = dot(d_ref[...], w_ref[...]) / n_ref[:, 0:1]
        high = pooled.astype(BF)
        low = (pooled - high.astype(F32)).astype(BF)
        dh_ref[...] = dot(p_ref[...], high, 0, 0) + dot(p_ref[...], low, 0, 0)
        up, down = gates(proj_ref, b_ref, units)
        up = (1.0 - up) * m_ref[:, 0:1]
        down = (1.0 - down) * m_ref[:, 1:2]
        store_scans(scan_pair(down, down * dh_ref[:, units:], up, up * dh_ref[:, :units]), outs)

    return call(run, (whole((chars, 2 * units), F32),) + scan_shapes(chars, units), "gru_back_open")(
        dfb, proj, bias, marks, pick, notes, w_charp_t
    )


def gru_back_close(scans, ends, d_hidden, proj, bias, marks, states, entries, w_recur):
    chars, units = scans[0].shape
    width = w_recur.shape[0]

    def run(
        cd, md, cu, mu, e0, e1, e2, e3, dh_ref, proj_ref, b_ref, m_ref, hu_ref, hd_ref, in_ref, w_ref,
        low_ref, high_ref, stat_ref, part_ref,
    ):
        from_below, from_above = entering((e0, e1, e2, e3))
        at = lax.broadcasted_iota(jnp.int32, (chars, units), 0)
        first, last = at == 0, at == chars - 1
        up, down = gates(proj_ref, b_ref, units)
        m = mu[...] + cu[...] * from_above
        lam = dh_ref[:, :units] + jnp.where(last, from_above, pltpu.roll(m, chars - 1, 0))
        before = jnp.where(first, in_ref[0:1], pltpu.roll(hu_ref[...], 1, 0))
        d_gate = lam * (proj_ref[:, units : 2 * units] - m_ref[:, 0:1] * before) * up * (1.0 - up)
        low_ref[:, :units] = d_gate.astype(BF)
        low_ref[:, units:] = (lam * up).astype(BF)
        stat_ref[...] = jnp.zeros(stat_ref.shape, F32)
        stat_ref[0:1, :units] = column_sum(d_gate)
        m = md[...] + cd[...] * from_below
        lam = dh_ref[:, units:] + jnp.where(first, from_below, pltpu.roll(m, 1, 0))
        beyond = jnp.where(last, in_ref[1:2], pltpu.roll(hd_ref[...], chars - 1, 0))
        d_gate = lam * (proj_ref[:, 3 * units :] - m_ref[:, 1:2] * beyond) * down * (1.0 - down)
        high_ref[:, :units] = d_gate.astype(BF)
        high_ref[:, units:] = (lam * down).astype(BF)
        stat_ref[1:2, :units] = column_sum(d_gate)
        part_ref[...] = dot(low_ref[...], w_ref[:, : 2 * units], 1, 1) + dot(high_ref[...], w_ref[:, 2 * units :], 1, 1)

    part = whole((chars, 2 * units), BF)
    return call(
        run, (part, part, whole((8, width), F32), whole((chars, width), F32)), "gru_back_close"
    )(*scans, *ends, d_hidden, proj, bias, marks, *states, *entries, w_recur)


def score_block(k, q, seg_k, seg_q):
    s = dot(k, q, 1, 1) * HD ** (-0.5)
    return jnp.where(seg_k == seg_q, s, MASKED_SCORE)


def attend(x, others, w_query, w_mix_t, seg_keys, seg_here):
    rows, width = x.shape
    half = w_mix_t.shape[1]
    heads = half // HD
    keys = rows * (1 + others.shape[0])

    def run(x_ref, o_ref, w_ref, wm_ref, sk_ref, sq_ref, q_ref, kv_ref, lse_ref, att_ref, part_ref, turned):
        q_ref[...] = dot(x_ref[...], w_ref[:, :half]).astype(BF)
        kv_ref[:rows] = dot(x_ref[...], w_ref[:, half:]).astype(BF)
        for m in range(others.shape[0]):
            kv_ref[(m + 1) * rows : (m + 2) * rows] = dot(o_ref[m], w_ref[:, half:]).astype(BF)
        lse_ref[...] = jnp.zeros(lse_ref.shape, F32)
        for h in range(heads):
            at = slice(h * HD, (h + 1) * HD)
            s = score_block(kv_ref[:, at], q_ref[:, at], sk_ref[...], sq_ref[...])
            highest = jnp.max(s, axis=0, keepdims=True)
            lse = highest + jnp.log(jnp.sum(jnp.exp(s - highest), axis=0, keepdims=True))
            lse_ref[h : h + 1] = lse
            probs = jnp.exp(s - lse).astype(BF)
            turned[at] = dot(kv_ref[:, half + h * HD : half + (h + 1) * HD], probs, 0, 0)
        att_ref[...] = turned[...].T.astype(BF)
        part_ref[...] = dot(att_ref[...], wm_ref[...], 1, 1)

    return call(
        run,
        (
            whole((rows, half), BF), whole((keys, 2 * half), BF), whole((8, rows), F32),
            whole((rows, half), BF), whole((rows, width), F32),
        ),
        "attend",
        (pltpu.VMEM((half, rows), F32),),
    )(x, others, w_query, w_mix_t, seg_keys, seg_here)


def attend_back(d_two, mine, other, n_one, inv_one, gains, w_mix_t, q, kv, lse, seg_keys, seg_here):
    rows, width = d_two.shape
    half = q.shape[1]
    heads = half // HD
    keys = kv.shape[0]
    count = keys // rows

    def run(
        d_ref, a_ref, b_ref, n_ref, i_ref, g_ref, wm_ref, q_ref, kv_ref, lse_ref, sk_ref, sq_ref,
        d1_ref, datt_ref, stat_ref, dq_ref, own_ref, s1_ref, s2_ref, s3_ref, da_ref, turned,
    ):
        e = d_ref[...] + (a_ref[...] + b_ref[...])
        n = n_ref[...]
        stat_ref[...] = jnp.zeros(stat_ref.shape, F32)
        stat_ref[0:1] = column_sum(e * n)
        stat_ref[1:2] = column_sum(e)
        d = row_norm_back(e, n, i_ref[...], g_ref[0:1])
        d1_ref[...] = d
        datt_ref[...] = d.astype(BF)
        da_ref[...] = dot(datt_ref[...], wm_ref[...]).astype(BF)
        scale = HD ** (-0.5)
        sends = (None, s1_ref, s2_ref, s3_ref)
        for h in range(heads):
            at = slice(h * HD, (h + 1) * HD)
            vt = slice(half + h * HD, half + (h + 1) * HD)
            s = score_block(kv_ref[:, at], q_ref[:, at], sk_ref[...], sq_ref[...])
            p = jnp.exp(s - lse_ref[h : h + 1])
            dp = dot(kv_ref[:, vt], da_ref[:, at], 1, 1)
            delta = jnp.sum(p * dp, axis=0, keepdims=True)
            ds = (p * (dp - delta)).astype(BF)
            turned[at] = dot(kv_ref[:, at], ds, 0, 0) * scale
            dk = dot(ds, q_ref[:, at]) * scale
            dv = dot(p.astype(BF), da_ref[:, at])
            own_ref[:, at] = dk[:rows]
            own_ref[:, vt] = dv[:rows]
            for m in range(1, count):
                sends[m][:, at] = dk[m * rows : (m + 1) * rows].astype(BF)
                sends[m][:, vt] = dv[m * rows : (m + 1) * rows].astype(BF)
        dq_ref[...] = turned[...].T.astype(BF)

    send = whole((rows, 2 * half), BF)
    return call(
        run,
        (
            whole((rows, width), F32), whole((rows, width), BF), whole((8, width), F32), whole((rows, half), BF),
            whole((rows, 2 * half), F32), send, send, send,
        ),
        "attend_back",
        (pltpu.VMEM((rows, half), BF), pltpu.VMEM((half, rows), F32)),
    )(d_two, mine, other, n_one, inv_one, gains, w_mix_t, q, kv, lse, seg_keys, seg_here)


def query_grads(x, d_att, att, dq, own, came, w_query):
    rows, width = x.shape
    half = att.shape[1]

    def run(x_ref, da_ref, att_ref, dq_ref, own_ref, c1, c2, c3, w_ref, o0, o1, o2, o3, part_ref, kv_ref):
        c = lax.axis_index(C)
        kv_ref[...] = (own_ref[...] + c1[...].astype(F32) + c2[...].astype(F32) + c3[...].astype(F32)).astype(BF)
        pairs = (
            (da_ref, att_ref[...]), (x_ref, dq_ref[...]), (x_ref, kv_ref[:, :half]), (x_ref, kv_ref[:, half:]),
        )
        for j, (left, right) in enumerate(pairs):
            grad = dot(left[...], right, 0, 0).astype(BF)
            for m, out in enumerate((o0, o1, o2, o3)):

                @pl.when(jnp.bitwise_xor(c, j) == m)
                def _():
                    out[...] = grad

        part_ref[...] = dot(dq_ref[...], w_ref[:, :half], 1, 1) + dot(kv_ref[...], w_ref[:, half:], 1, 1)

    return call(
        run,
        (whole((width, half), BF),) * 4 + (whole((rows, width), F32),),
        "query_grads",
        (pltpu.VMEM((rows, 2 * half), BF),),
    )(x, d_att, att, dq, own, *came, w_query)


def gelu_parts(x):
    cdf = 0.5 * (1.0 + lax.erf(x * 0.7071067811865476))
    return cdf, jnp.exp(-0.5 * x * x) * 0.3989422804014327


def feed(x, mine, other, gains, shifts, w_upper, w_lower_t):
    rows, width = x.shape
    hidden = w_upper.shape[1]

    def run(x_ref, a_ref, b_ref, g_ref, s_ref, wu_ref, wd_ref, n_ref, i_ref, low_ref, pre_ref, act_ref, part_ref):
        n, inverse = row_norm(x_ref[...].astype(F32) + (a_ref[...] + b_ref[...]))
        n_ref[...] = n
        i_ref[...] = inverse
        low_ref[...] = (n * g_ref[0:1] + s_ref[0:1]).astype(BF)
        step = hidden // 4
        total = jnp.zeros((rows, width), F32)
        for i in range(4):
            at = slice(i * step, (i + 1) * step)
            pre = dot(low_ref[...], wu_ref[:, at])
            pre_ref[:, at] = pre
            act_ref[:, at] = (pre * gelu_parts(pre)[0]).astype(BF)
            total += dot(act_ref[:, at], wd_ref[:, at], 1, 1)
        part_ref[...] = total

    return call(
        run,
        (
            whole((rows, width), F32), whole((rows, 1), F32), whole((rows, width), BF), whole((rows, hidden), F32),
            whole((rows, hidden), BF), whole((rows, width), F32),
        ),
        "feed",
    )(x, mine, other, gains, shifts, w_upper, w_lower_t)


def feed_close(n_one, mine, other, gains, shifts, w_token):
    rows, width = n_one.shape
    half = w_token.shape[1]

    def run(n1_ref, a_ref, b_ref, g_ref, s_ref, w_ref, n_ref, i_ref, x2_ref, low_ref, fa_ref):
        first = n1_ref[...] * g_ref[0:1] + s_ref[0:1]
        n, inverse = row_norm(first + (a_ref[...] + b_ref[...]))
        n_ref[...] = n
        i_ref[...] = inverse
        second = n * g_ref[1:2] + s_ref[1:2]
        x2_ref[...] = second
        low_ref[...] = second.astype(BF)
        fa_ref[...] = dot(low_ref[...], w_ref[...]).astype(BF)

    return call(
        run,
        (
            whole((rows, width), F32), whole((rows, 1), F32), whole((rows, width), F32), whole((rows, width), BF),
            whole((rows, half), BF),
        ),
        "feed_close",
    )(n_one, mine, other, gains, shifts, w_token)


def join_back(parts, w_token):
    rows, half = parts[0].shape
    width = w_token.shape[0]

    def run(*refs):
        w_ref, low_ref, part_ref = refs[len(parts) :]
        total = refs[0][...].astype(F32)
        for ref in refs[1 : len(parts)]:
            total = total + ref[...].astype(F32)
        low_ref[...] = total.astype(BF)
        part_ref[...] = dot(low_ref[...], w_ref[...], 1, 1)

    return call(run, (whole((rows, half), BF), whole((rows, width), F32)), "join_back")(*parts, w_token)


def feed_back(d_three, mine, other, n_two, inv_two, gains, pre, w_upper, w_lower_t):
    rows, width = d_three.shape
    hidden = pre.shape[1]

    def run(d_ref, a_ref, b_ref, n_ref, i_ref, g_ref, pre_ref, wu_ref, wd_ref, d2_ref, low_ref, dpre_ref, part_ref, stat_ref):
        e = d_ref[...] + (a_ref[...] + b_ref[...])
        n = n_ref[...]
        stat_ref[...] = jnp.zeros(stat_ref.shape, F32)
        stat_ref[0:1] = column_sum(e * n)
        stat_ref[1:2] = column_sum(e)
        d = row_norm_back(e, n, i_ref[...], g_ref[1:2])
        d2_ref[...] = d
        low_ref[...] = d.astype(BF)
        step = hidden // 4
        total = jnp.zeros((rows, width), F32)
        for i in range(4):
            at = slice(i * step, (i + 1) * step)
            x = pre_ref[:, at]
            cdf, pdf = gelu_parts(x)
            dpre_ref[:, at] = (dot(low_ref[...], wd_ref[:, at]) * (cdf + x * pdf)).astype(BF)
            total += dot(dpre_ref[:, at], wu_ref[:, at], 1, 1)
        part_ref[...] = total

    return call(
        run,
        (
            whole((rows, width), F32), whole((rows, width), BF), whole((rows, hidden), BF), whole((rows, width), F32),
            whole((8, width), F32),
        ),
        "feed_back",
    )(d_three, mine, other, n_two, inv_two, gains, pre, w_upper, w_lower_t)


def neighbours(x):
    return [x] + [swap(x, C, m) for m in (1, 2, 3)]


def body(
    tokens_in, chars_in, segment_ids, char_counts, valid, teacher_tokens, teacher_chars,
    w_qkv, w_out, w_up, w_down, w_gru, gru_bias, w_tok, w_char, w_conv, ln_gain, ln_bias,
):
    nz = lax.axis_size(Z)
    c = lax.axis_index(C)
    t = lax.axis_index(T)
    rows, width = tokens_in.shape
    chars = chars_in.shape[0]
    half = width // 2
    units = gru_bias.shape[2]
    shard = w_qkv.shape[1]
    hidden = w_up.shape[2]
    gains, shifts, bias = ln_gain[0], ln_bias[0], gru_bias[0]

    mine = own_part(tokens_in, 2, t)
    others = core_join(jnp.stack([swap(mine, C, m) for m in (1, 2, 3)]), 1)
    widths = ((3 * half, 4 * units, half, half), (hidden, half, hidden))
    shards = (
        jnp.concatenate(
            [w_qkv[0].reshape(shard, -1), w_gru[0].reshape(shard, -1), w_char[0].reshape(-1, shard).T, w_out[0].T], axis=1
        ),
        jnp.concatenate([w_up[0], w_tok[0], w_down[0].T], axis=1),
    )
    quartered = shard % 64 == 0
    if quartered:
        stacks = [gather_beside(context_quarter(x), 1) for x in shards]
        firsts, nears = first_round(stacks[0][:, :, : shards[0].shape[1]], (others,))
        fars = second_round(firsts, nears)
        stacks[1] = after(stacks[1], fars)
        w_query, w_recur, w_charp_t, w_mix_t = assemble(shards[0], list(zip(firsts, nears, fars)), widths[0])
        firsts, nears = first_round(stacks[1][:, :, : shards[1].shape[1]], ())
    else:
        full = [lax.all_gather(x, Z, axis=0, tiled=True) for x in shards]
        w_query, w_recur, w_charp_t, w_mix_t = jnp.split(full[0], [3 * half, 3 * half + 4 * units, 4 * half + 4 * units], axis=1)
    seq_len = segment_ids.shape[1]
    offset_here = c * rows
    seg_full = segment_ids[0]
    seg_here = lax.dynamic_slice_in_dim(seg_full, offset_here, rows)
    seg_keys = jnp.concatenate(
        [lax.dynamic_slice_in_dim(seg_full, jnp.bitwise_xor(c, m) * rows, rows) for m in range(4)]
    )[:, None]
    counts = char_counts[0]
    ends = jnp.cumsum(counts)
    starts = ends - counts
    places = jnp.arange(chars, dtype=jnp.int32)
    chosen = jnp.logical_and(starts[:, None] <= places[None, :], places[None, :] < ends[:, None])
    pick = chosen.astype(BF)
    valid_tok = valid[0].astype(F32)
    char_seg = jnp.sum(jnp.where(chosen, seg_here[:, None], 0), axis=0)
    valid_chr = jnp.sum(jnp.where(chosen, valid_tok[:, None], 0.0), axis=0)
    prev_seg = seg_full[jnp.maximum(offset_here - 1, 0)]
    next_seg = seg_full[jnp.minimum(offset_here + rows, seq_len - 1)]
    first_keep = jnp.logical_and(c > 0, prev_seg == char_seg[0])
    last_keep = jnp.logical_and(c < lax.axis_size(C) - 1, next_seg == char_seg[-1])
    same = char_seg[1:] == char_seg[:-1]
    keep_up = jnp.concatenate([first_keep[None], same]).astype(F32)
    keep_down = jnp.concatenate([same, last_keep[None]]).astype(F32)
    marks = jnp.stack([keep_up, keep_down, valid_chr], axis=1)
    notes = jnp.stack([counts.astype(F32), valid_tok], axis=1)
    seg_row = seg_here[None, :]

    proj, *scans, ends_here = gru_open(chars_in, w_recur, bias, marks)
    ends_all = neighbours(ends_here)
    if quartered:
        fars = second_round(firsts, nears, ends_all[1:])
    *states, entries, pooled_low, keep, send = gru_close(
        scans, ends_all, pick, after(notes, nears) if quartered else notes, w_charp_t
    )
    fb = (keep + swap(send, T, 1)).astype(BF)
    fbs = gather_beside(fb, 0)

    q, kv, lse, mixed_low, part = attend(after(tokens_in, fb), others, w_query, w_mix_t, seg_keys, seg_row)
    if quartered:
        fars = after(fars, part)
        w_upper, w_token, w_lower_t = assemble(shards[1], list(zip(firsts, nears, fars)), widths[1])
    else:
        w_upper, w_token, w_lower_t = jnp.split(full[1], [hidden, hidden + half], axis=1)
    n_one, inv_one, first_low, pre, act_low, part2 = feed(
        after(tokens_in, fbs), part, swap(part, T, 1), gains, shifts, w_upper, w_lower_t
    )
    gathered = lax.all_gather(jnp.concatenate([own_part(first_low, 2, t, 1), act_low], axis=1), C)
    n_two, inv_two, second, second_low, fa = feed_close(n_one, part2, swap(part2, T, 1), gains, shifts, w_token)
    ends_u = [jnp.concatenate([fa[at], fb[at]]) for at in (slice(0, 1), slice(rows - 1, rows))]
    before, beyond = from_neighbours(*ends_u)
    rim = jnp.concatenate([before[:1], beyond[:1], before[1:], beyond[1:], jnp.zeros((12, half), BF)])
    fas = turned_all(jnp.concatenate([fa, rim]))

    cols = w_conv.shape[-1]
    kernel = w_conv[0].reshape(3, width, cols)
    keep, send = conv_main(fas, fbs, kernel)
    conv = add_split(keep, swap(send, T, 1))
    y_half = side_by_side([conv[0]] + [turn(conv[k], Z, nz - k) for k in range(1, nz)], True)
    out_tok, out_chr, d_res_three, d_res_four, d_mine, stats = close(
        second, y_half, swap(y_half, T, 1), chars_in, teacher_tokens, teacher_chars, pick,
        notes, marks, gains, shifts,
    )

    before, beyond = from_neighbours(d_mine[:1], d_mine[-1:])
    rim = jnp.where(t == 0, beyond, before)
    d_mine = jnp.concatenate([d_mine, rim, jnp.zeros((15, 2 * width), BF)])
    slices = column_slices(d_mine, nz)
    dy_mine = jnp.stack([slices[0]] + [turn(slices[k], Z, k) for k in range(1, nz)])
    dy_other = swap(dy_mine, T, 1)
    du_tok, du_chr = conv_back(after(dy_mine, gathered), dy_other, kernel)
    grad_kernel = conv_grads(fas, fbs, dy_mine, dy_other)
    tok_came = after([turn(du_tok[k], Z, nz - k) for k in range(1, nz)], grad_kernel)
    chr_came = [turn(after(du_chr[k], grad_kernel), Z, nz - k) for k in range(1, nz)]
    dfa, part = join_back([du_tok[0]] + tok_came, w_token)
    grad_kernel = lax.psum_scatter(grad_kernel, C, scatter_dimension=0)

    d_res_two, d_ffn, d_pre, part, stats_two = feed_back(
        d_res_three, part, swap(part, T, 1), n_two, inv_two, gains, pre, w_upper, w_lower_t
    )

    dfb = summed(du_chr[0], after(chr_came, d_pre))
    dfb_full = core_join(dfb, 1)
    d_hidden, *scans, ends_here = gru_back_open(dfb_full, proj, bias, marks, pick, notes, w_charp_t)
    ends_all = neighbours(ends_here)
    pre_own, pre_came = exchange(d_ffn, d_pre, ends_all[1:])
    gathered = [lax.dynamic_index_in_dim(gathered, jnp.bitwise_xor(c, m), 0, keepdims=False) for m in range(4)]
    act_part = jnp.concatenate([own_part(x[:, half:], 4, c, 1) for x in gathered])
    first_all = core_join(jnp.concatenate([x[:, :half] for x in gathered]), 1)
    d_low, d_high, stats_bias, part_chr = gru_back_close(
        scans, ends_all, d_hidden, proj, bias, marks, states, (entries,), w_recur
    )
    d_chr_in = d_res_four + core_sum(part_chr)
    sent = sent_apart(((second_low, dfa), (dfb_full, pooled_low), (chars_in, d_low), (chars_in, d_high)), 1, None)
    chars_own, *chars_sent = sent

    grad_kernel = lax.all_gather(grad_kernel, C)

    pre_came = after(pre_came, chars_sent)
    chars_came = [swap(x, C, m) for m, x in zip((1, 2, 3), chars_sent)]
    d_res_one, d_att, stats_one, dq, dkv_own, *dkv_sends = attend_back(
        after(d_res_two, pre_came), part, swap(part, T, 1), n_one, inv_one, gains, w_mix_t, q, kv, lse, seg_keys, seg_row
    )
    came = [swap(x, C, m) for m, x in zip((1, 2, 3), dkv_sends)]
    ffn_all, pre_part = collected(d_ffn, pre_own, after(pre_came, dq))
    g_up = dot(first_all, pre_part, 0, 0).astype(BF)
    g_down = dot(ffn_all, act_part, 0, 0).astype(BF)
    ffn_piece = lax.psum_scatter(jnp.concatenate([g_up, g_down], axis=1), Z, scatter_dimension=0, tiled=True)
    chars_came = after(chars_came, dq)
    chars_piece = lax.psum_scatter(summed(chars_own, chars_came), Z, scatter_dimension=0, tiled=True)

    counted = jnp.full((1, width), jnp.sum(valid_tok))
    packed = jnp.concatenate([stats[:5], counted, stats_bias[:2], stats_one[:2], stats_two[:2]])
    packed = after(packed, chars_came)
    packed = packed + swap(packed, C, 1)

    *sent, part = query_grads(tokens_in, d_att, mixed_low, dq, dkv_own, came, w_query)
    query_own, *query_sent = sent
    query_came = [swap(x, C, m) for m, x in zip((1, 2, 3), query_sent)]
    d_tok_in = d_res_one + core_sum(part)
    query_blocks = z_split([query_own] + query_came)
    query_turned = turned(query_blocks)
    copies = lax.all_gather(jnp.concatenate(after([ffn_piece, chars_piece], query_sent), axis=1), C)
    copies = after(copies, query_blocks)
    grad_kernel = after(grad_kernel, query_blocks).reshape(2, 2, 3, half // 2, cols).astype(F32)
    grad_kernel = grad_kernel.transpose(2, 0, 1, 3, 4)
    g_up, g_down, g_tok, g_char, g_gru = early_join(copies)
    query_turned = after(query_turned, g_up)
    query_piece = summed(query_blocks[0], query_turned)
    g_out, g_query = query_join([query_piece] + swapped(query_piece))

    packed = after(packed, query_sent)
    packed = packed + swap(packed, C, 2)
    bit = 1
    while bit < nz:
        packed = packed + swap(packed, Z, bit)
        bit *= 2
    loss = jnp.sum(packed[4]) / packed[5, 0]
    gain_total = jnp.stack([packed[8], packed[10], packed[0], packed[1]])[None]
    shift_total = jnp.stack([packed[9], packed[11], packed[2], packed[3]])[None]
    bias_total = packed[None, 6:8, :units]
    return (
        out_tok,
        out_chr,
        loss,
        d_tok_in,
        d_chr_in,
        g_query[None],
        g_out[None],
        g_up[None],
        g_down[None],
        g_gru.reshape(w_gru.shape),
        bias_total,
        g_tok[None],
        g_char.reshape(w_char.shape),
        grad_kernel.reshape(w_conv.shape),
        gain_total,
        shift_total,
    )


def solution(mesh):
    tok = P((Z, C), None)
    seq = P(Z, None)
    placed = (
        tok, tok, seq, tok, P(Z, C), tok, tok,
        P(None, Z, None, T), P(None, T, Z), P(None, Z, T), P(None, T, Z), P(None, Z, None, T),
        P(None, None, T), P(None, Z, T), P(None, None, T, Z), P(None, None, None, T, Z), P(), P(),
    )
    given = (
        tok, tok, P(), tok, tok,
        P(None, Z, None, T), P(None, T, Z), P(None, Z, T), P(None, T, Z), P(None, Z, None, T),
        P(None, None, T), P(None, Z, T), P(None, None, T, Z), P(None, None, None, T, Z), P(), P(),
    )
    return jax.shard_map(body, mesh=mesh, in_specs=placed, out_specs=given, check_vma=False)
```

profile of v0, /device:TPU:0, one launch (start us, length us, event | category | flops | bytes accessed | tf_op | source)
XLA Modules:
  0.0 496.8 jit_solution(18036625217776139937)
XLA Ops:
  19.1 4.8 collective-permute-done.1
  27.2 14.3 %all-gather.14.cloned.1.call-done = bf16[192,2816]{1,0:T(8,128)(2,1)} async-done(((bf16[48,2816]{1,0:T(8,128)(2,1)}), bf16[192,2816]{1,0:T(8,128)(2,1)}) %all-gather.14.cloned.1.call-update) | async-done | bytes 1081360 | tf_op jit(solution)/shard_map/all_gather | solution.py:290
  46.9 6.4 %collective-permute-done.4.refs_1_ = bf16[3,48,1280]{2,1,0:T(8,128)(2,1)S(1)} collective-permute-done((bf16[3,48,1280]{2,1,0:T(8,128)(2,1)S(1)}, bf16[3,48,1280]{2,1,0:T(8,128)(2,1)S(1)}, u32[]{:S(2)}, u32[]{:S(2)}) %collective-permute-start.4) | collective-permute-done | bytes 368672 | tf_op jit(solution)/shard_map/ppermute | solution.py:27
  66.7 9.5 %all-gather.16.cloned.1.call-done = bf16[192,3456]{1,0:T(8,128)(2,1)} async-done(((bf16[48,3456]{1,0:T(8,128)(2,1)}), bf16[192,3456]{1,0:T(8,128)(2,1)}) %all-gather.16.cloned.1.call-update) | async-done | bytes 1327120 | tf_op jit(solution)/shard_map/all_gather | solution.py:290
  86.5 4.7 gru_open.1
  109.5 10.6 %attend.1 = (bf16[256,384]{1,0:T(8,128)(2,1)}, bf16[1024,768]{1,0:T(8,128)(2,1)}, f32[8,256]{1,0:T(8,128)}, bf16[256,384]{1,0:T(8,128)(2,1)}, f32[256,768]{1,0:T(8,128)}) custom-call(bf16[256,768]{1,0:T(8,128)(2,1)} %x_ref.3, bf16[3,256,768]{2,1,0:T(8,128)(2,1)} %pad_maximum_fusion.1.o_ref, bf16[768,1152]{1,0:T(8,128)(2,1)} %get-tuple-element.171.w_ref, ...), custom_call_target="tpu_custom_call" | custom-call | flops 1 | bytes 1 | tf_op jit(solution)/shard_map/attend/pallas_call | solution.py:723
  120.1 10.0 %collective-permute-done.15.refs_2_ = bf16[6,48,1664]{2,1,0:T(8,128)(2,1)S(1)} collective-permute-done((bf16[6,48,1664]{2,1,0:T(8,128)(2,1)}, bf16[6,48,1664]{2,1,0:T(8,128)(2,1)S(1)}, u32[]{:S(2)}, u32[]{:S(2)}) %collective-permute-start.15) | collective-permute-done | bytes 958496 | tf_op jit(solution)/shard_map/ppermute | solution.py:27
  131.1 5.3 %assemble.3 = (bf16[768,1536]{1,0:T(8,128)(2,1)}, bf16[768,384]{1,0:T(8,128)(2,1)}, bf16[768,1536]{1,0:T(8,128)(2,1)}) custom-call(bf16[3,48,1664]{2,1,0:T(8,128)(2,1)} %copy-done.4, bf16[3,48,1664]{2,1,0:T(8,128)(2,1)} %copy-done.10, bf16[6,48,1664]{2,1,0:T(8,128)(2,1)} %copy-done.19, bf16[3,48,1792]{2,1,0:T(8,128)(2,1)} %copy-done.3, ...), custom_call_target="tpu_custom_call" | custom-call | flops 1 | bytes 1 | tf_op jit(solution)/shard_map/assemble/pallas_call | solution.py:122
  137.3 6.7 %feed.1 = (f32[256,768]{1,0:T(8,128)}, f32[256,1]{1,0:T(8,128)}, bf16[256,768]{1,0:T(8,128)(2,1)}, f32[256,1536]{1,0:T(8,128)}, bf16[256,1536]{1,0:T(8,128)(2,1)}, /*index=5*/f32[256,768]{1,0:T(8,128)}) custom-call(bf16[256,768]{1,0:T(8,128)(2,1)} %x_ref.3, f32[256,768]{1,0:T(8,128)} %get-tuple-element.173.a_ref, f32[256,768]{1,0:T(8,128)} %copy-done.24, ...), custom_call_target="tpu_custom_call" | custom-call | flops 1 | bytes 1 | tf_op jit(solution)/shard_map/feed/pallas_call | solution.py:838
  166.5 5.6 %collective-permute-done.20.refs_1_ = bf16[272,384]{1,0:T(8,128)(2,1)S(1)} collective-permute-done((bf16[272,384]{1,0:T(8,128)(2,1)S(1)}, bf16[272,384]{1,0:T(8,128)(2,1)S(1)}, u32[]{:S(2)}, u32[]{:S(2)}) %collective-permute-start.20) | collective-permute-done | bytes 208928 | tf_op jit(solution)/shard_map/ppermute | solution.py:32
  172.1 6.8 %collective-permute-done.21.refs_2_ = bf16[272,384]{1,0:T(8,128)(2,1)S(1)} collective-permute-done((bf16[272,384]{1,0:T(8,128)(2,1)S(1)}, bf16[272,384]{1,0:T(8,128)(2,1)S(1)}, u32[]{:S(2)}, u32[]{:S(2)}) %collective-permute-start.21) | collective-permute-done | bytes 208928 | tf_op jit(solution)/shard_map/ppermute | solution.py:32
  179.7 7.6 %conv.1 = (f32[4,128,384]{2,1,0:T(8,128)}, f32[4,128,384]{2,1,0:T(8,128)}) custom-call(bf16[272,384]{1,0:T(8,128)(2,1)} %copy-done.11, bf16[272,384]{1,0:T(8,128)(2,1)} %copy-done.20, bf16[272,384]{1,0:T(8,128)(2,1)} %copy-done.21, bf16[272,384]{1,0:T(8,128)(2,1)} %copy-done.22, bf16[4,352,384]{2,1,0:T(8,128)(2,1)} %bitcast.100, bf16[3,768,384]{2,1,0:T(8,128)(2,1)} %bitcast.98), custom_call_target="tpu_custom_call" | custom-call | flops 1 | bytes 1 | tf_op jit(solution)/shard_map/conv/pallas_call | solution.py:348
  192.8 4.8 collective-permute-start.24
  201.1 6.9 %collective-permute-done.25.refs_2_ = bf16[128,384]{1,0:T(8,128)(2,1)S(1)} collective-permute-done((bf16[128,384]{1,0:T(8,128)(2,1)}, bf16[128,384]{1,0:T(8,128)(2,1)S(1)}, u32[]{:S(2)}, u32[]{:S(2)}) %collective-permute-start.25) | collective-permute-done | bytes 98336 | tf_op jit(solution)/shard_map/ppermute | solution.py:32
  213.2 5.6 %close.1 = (f32[256,768]{1,0:T(8,128)}, f32[384,768]{1,0:T(8,128)}, f32[256,768]{1,0:T(8,128)}, f32[384,768]{1,0:T(8,128)}, bf16[128,1536]{1,0:T(8,128)(2,1)}, /*index=5*/f32[8,768]{1,0:T(8,128)}) custom-call(f32[256,768]{1,0:T(8,128)} %get-tuple-element.183.s_ref, bf16[128,1536]{1,0:T(8,128)(2,1)} %side_by_side.1.ym_ref, bf16[128,1536]{1,0:T(8,128)(2,1)} %copy-done.41, ...), custom_call_target="tpu_custom_call" | custom-call | flops 1 | bytes 1 | tf_op jit(solution)/shard_map/close/pallas_call | solution.py:458
  239.2 5.9 %conv_back.1 = (bf16[256,384]{1,0:T(8,128)(2,1)}, bf16[256,384]{1,0:T(8,128)(2,1)}, bf16[256,384]{1,0:T(8,128)(2,1)}, bf16[256,384]{1,0:T(8,128)(2,1)}, bf16[256...) custom-call(bf16[4,144,384]{2,1,0:T(8,128)(2,1)} %copy-done.5, ...), custom_call_target="tpu_custom_call" | custom-call | flops 1 | bytes 1 | tf_op jit(solution)/shard_map/conv_back/pallas_call | solution.py:512
  248.6 6.1 %conv_grads.1 = bf16[4,3,192,384]{3,2,1,0:T(8,128)(2,1)} custom-call(bf16[272,384]{1,0:T(8,128)(2,1)} %copy-done.11, bf16[272,384]{1,0:T(8,128)(2,1)} %copy-done.20, bf16[272,384]{1,0:T(8,128)(2,1)} %copy-done.21, bf16[272,384]{1,0:T(8,128)(2,1)} %copy-done.22, bf16[4,352,384]{2,1,0:T(8,128)(2,1)} %bitcast.101, bf16[4,144,384]{2,1,0:T(8,128)(2,1)} %copy-done.5, ...), custom_call_target="tpu_custom_call" | custom-call | flops 1 | bytes 1 | tf_op jit(solution)/shard_map/conv_grads/pallas_call | solution.py:534
  254.7 11.5 %collective-permute-done.38.refs_2_ = bf16[256,384]{1,0:T(8,128)(2,1)S(1)} collective-permute-done((bf16[256,384]{1,0:T(8,128)(2,1)}, bf16[256,384]{1,0:T(8,128)(2,1)S(1)}, u32[]{:S(2)}, u32[]{:S(2)}) %collective-permute-start.38) | collective-permute-done | bytes 196640 | tf_op jit(solution)/shard_map/ppermute | solution.py:32
  274.7 7.1 %feed_back.1 = (f32[256,768]{1,0:T(8,128)}, bf16[256,768]{1,0:T(8,128)(2,1)}, bf16[256,1536]{1,0:T(8,128)(2,1)}, f32[256,768]{1,0:T(8,128)}, f32[8,768]{1,0:T(8,128)}) custom-call(f32[256,768]{1,0:T(8,128)} %get-tuple-element.205.d_ref, f32[256,768]{1,0:T(8,128)} %get-tuple-element.213.a_ref, f32[256,768]{1,0:T(8,128)} %copy-done.25, ...), custom_call_target="tpu_custom_call" | custom-call | flops 1 | bytes 1 | tf_op jit(solution)/shard_map/feed_back/pallas_call | solution.py:910
  281.9 5.0 %collective-permute-done.35 = bf16[256,384]{1,0:T(8,128)(2,1)S(1)} collective-permute-done((bf16[256,384]{1,0:T(8,128)(2,1)S(1)}, bf16[256,384]{1,0:T(8,128)(2,1)S(1)}, u32[]{:S(2)}, u32[]{:S(2)}) %collective-permute-start.35) | collective-permute-done | bytes 196640 | tf_op jit(solution)/shard_map/ppermute | solution.py:32
  305.5 5.2 %gru_back_close.1 = (bf16[384,384]{1,0:T(8,128)(2,1)}, bf16[384,384]{1,0:T(8,128)(2,1)}, f32[8,768]{1,0:T(8,128)}, f32[384,768]{1,0:T(8,128)}) custom-call(f32[384,192]{1,0:T(8,128)} %get-tuple-element.222.cd, f32[384,192]{1,0:T(8,128)} %get-tuple-element.223.md, f32[384,192]{1,0:T(8,128)} %get-tuple-element.224.cu, f32[384,192]{1,0:T(8,128)} %get-tuple-element.225.mu, ...), custom_call_target="tpu_custom_call" | custom-call | flops 1 | bytes 1 | tf_op jit(solution)/shard_map/gru_back_close/pallas_call | solution.py:690
  310.7 5.6 %grads.1 = (bf16[768,384]{1,0:T(8,128)(2,1)}, bf16[768,384]{1,0:T(8,128)(2,1)}, bf16[768,384]{1,0:T(8,128)(2,1)}, bf16[768,384]{1,0:T(8,128)(2,1)}) custom-call(bf16[256,768]{1,0:T(8,128)(2,1)} %get-tuple-element.235.refs_0_, bf16[256,384]{1,0:T(8,128)(2,1)} %get-tuple-element.236.refs_1_, bf16[256,768]{1,0:T(8,128)(2,1)} %pad_maximum_fusion.22.d_ref.refs_2_, ...), custom_call_target="tpu_custom_call" | custom-call | flops 1 | bytes 1 | tf_op jit(solution)/shard_map/grads/pallas_call | solution.py:172
  316.3 5.3 %collective-permute-done.47 = bf16[512,384]{1,0:T(8,128)(2,1)S(1)} collective-permute-done((bf16[512,384]{1,0:T(8,128)(2,1)S(1)}, bf16[512,384]{1,0:T(8,128)(2,1)S(1)}, u32[]{:S(2)}, u32[]{:S(2)}) %collective-permute-start.47) | collective-permute-done | bytes 393248 | tf_op jit(solution)/shard_map/ppermute | solution.py:27
  322.5 10.7 %attend_back.1 = (f32[256,768]{1,0:T(8,128)}, bf16[256,768]{1,0:T(8,128)(2,1)}, f32[8,768]{1,0:T(8,128)}, bf16[256,384]{1,0:T(8,128)(2,1)}, f32[256,768]{1,0:T(8...) custom-call(f32[256,768]{1,0:T(8,128)} %get-tuple-element.246.d_ref, ...), custom_call_target="tpu_custom_call" | custom-call | flops 1 | bytes 1 | tf_op jit(solution)/shard_map/attend_back/pallas_call | solution.py:775
  341.8 12.7 %collective-permute-done.49 = bf16[768,384]{1,0:T(8,128)(2,1)S(1)} collective-permute-done((bf16[768,384]{1,0:T(8,128)(2,1)S(1)}, bf16[768,384]{1,0:T(8,128)(2,1)S(1)}, u32[]{:S(2)}, u32[]{:S(2)}) %collective-permute-start.49) | collective-permute-done | bytes 589856 | tf_op jit(solution)/shard_map/ppermute | solution.py:27
  354.5 12.2 %collective-permute-done.50 = bf16[768,384]{1,0:T(8,128)(2,1)S(1)} collective-permute-done((bf16[768,384]{1,0:T(8,128)(2,1)S(1)}, bf16[768,384]{1,0:T(8,128)(2,1)S(1)}, u32[]{:S(2)}, u32[]{:S(2)}) %collective-permute-start.50) | collective-permute-done | bytes 589856 | tf_op jit(solution)/shard_map/ppermute | solution.py:27
  372.5 8.6 %collective-permute-done.53.c1 = bf16[256,768]{1,0:T(8,128)(2,1)S(1)} collective-permute-done((bf16[256,768]{1,0:T(8,128)(2,1)S(1)}, bf16[256,768]{1,0:T(8,128)(2,1)S(1)}, u32[]{:S(2)}, u32[]{:S(2)}) %collective-permute-start.53) | collective-permute-done | bytes 393248 | tf_op jit(solution)/shard_map/ppermute | solution.py:27
  381.1 5.8 %collective-permute-done.54.c2 = bf16[256,768]{1,0:T(8,128)(2,1)S(1)} collective-permute-done((bf16[256,768]{1,0:T(8,128)(2,1)S(1)}, bf16[256,768]{1,0:T(8,128)(2,1)S(1)}, u32[]{:S(2)}, u32[]{:S(2)}) %collective-permute-start.54) | collective-permute-done | bytes 393248 | tf_op jit(solution)/shard_map/ppermute | solution.py:27
  389.1 6.5 %query_grads.1 = (bf16[768,384]{1,0:T(8,128)(2,1)}, bf16[768,384]{1,0:T(8,128)(2,1)}, bf16[768,384]{1,0:T(8,128)(2,1)}, bf16[768,384]{1,0:T(8,128)(2,1)}, f32[256,768]{1,0:T(8,128)}) custom-call(bf16[256,768]{1,0:T(8,128)(2,1)} %x_ref.3, bf16[256,768]{1,0:T(8,128)(2,1)} %get-tuple-element.259.da_ref, bf16[256,384]{1,0:T(8,128)(2,1)} %get-tuple-element.260.att_ref, ...), custom_call_target="tpu_custom_call" | custom-call | flops 1 | bytes 1 | tf_op jit(solution)/shard_map/query_grads/pallas_call | solution.py:806
  429.3 7.7 %collective-permute-done.61.refs_1_ = bf16[768,384]{1,0:T(8,128)(2,1)} collective-permute-done((bf16[768,384]{1,0:T(8,128)(2,1)}, bf16[768,384]{1,0:T(8,128)(2,1)}, u32[]{:S(2)}, u32[]{:S(2)}) %collective-permute-start.61) | collective-permute-done | bytes 589856 | tf_op jit(solution)/shard_map/ppermute | solution.py:27
  436.9 17.1 %collective-permute-done.63.refs_3_ = bf16[768,384]{1,0:T(8,128)(2,1)} collective-permute-done((bf16[768,384]{1,0:T(8,128)(2,1)}, bf16[768,384]{1,0:T(8,128)(2,1)}, u32[]{:S(2)}, u32[]{:S(2)}) %collective-permute-start.63) | collective-permute-done | bytes 589856 | tf_op jit(solution)/shard_map/ppermute | solution.py:27
  462.9 4.7 all-gather.22.cloned.1.call-done
  (453 shorter events, 228.9 us)
Async XLA Ops:
  7.2 34.3 %all-gather.14.cloned.1.call-start = ((), (), s32[]{:S(2)}) async-start(), calls=%async_computation.5 | async-start | bytes 1351680 | tf_op jit(solution)/shard_map/all_gather | solution.py:290
  10.2 66.0 %all-gather.16.cloned.1.call-start = ((), (), s32[]{:S(2)}) async-start(), calls=%async_computation.6 | async-start | bytes 1658880 | tf_op jit(solution)/shard_map/all_gather | solution.py:290
  24.8 111.6 %all-gather.18.cloned.1.call-start = ((), (), s32[]{:S(2)}) async-start(), calls=%async_computation.7 | async-start | bytes 1351680 | tf_op jit(solution)/shard_map/all_gather | solution.py:290
  54.2 22.0 %collective-permute-start.5 = (bf16[6,48,1280]{2,1,0:T(8,128)(2,1)}, bf16[6,48,1280]{2,1,0:T(8,128)(2,1)S(1)}, u32[]{:S(2)}, u32[]{:S(2)}) collective-permute-start(bf16[6,48,1280]{2,1,0:T(8,128)(2,1)} %pad_maximum_fusion.9), channel_id=1, source_target_pairs={{0,4},{2,6},{4,0},{6,2},{1,5},{3,7},{5,1},{7,3},{8,12},{10,14},{12... | collective-permute-start | bytes 2211848 | tf_op jit(solution)/shard_map/ppermute | solution.py:27
  55.8 20.4 %collective-permute-start.7 = (bf16[6,48,1408]{2,1,0:T(8,128)(2,1)S(1)}, bf16[6,48,1408]{2,1,0:T(8,128)(2,1)S(1)}, u32[]{:S(2)}, u32[]{:S(2)}) collective-permute-start(bf16[6,48,1408]{2,1,0:T(8,128)(2,1)S(1)} %pad_maximum_fusion.7), channel_id=1, source_target_pairs={{0,2},{2,0},{4,6},{6,4},{1,3},{3,1},{5,7},{7,5},{8,10},{10,8},{12,... | collective-permute-start | bytes 2433032 | tf_op jit(solution)/shard_map/ppermute | solution.py:27
  78.2 16.5 %collective-permute-start.12 = (bf16[3,48,1792]{2,1,0:T(8,128)(2,1)S(1)}, bf16[3,48,1792]{2,1,0:T(8,128)(2,1)S(1)}, u32[]{:S(2)}, u32[]{:S(2)}) collective-permute-start(bf16[3,48,1792]{2,1,0:T(8,128)(2,1)S(1)} %pad_maximum_fusion.13.refs_3_), channel_id=1, source_target_pairs={{0,4},{2,6},{4,0},{6,2},{1,5},{3,7},{5,1},{7,3},{8,12},{10,14},{12... | collective-permute-start | bytes 1548296 | tf_op jit(solution)/shard_map/ppermute | solution.py:27
  104.9 131.8 %all-gather.20.cloned.1.call-start = ((), (), s32[]{:S(2)}) async-start(), calls=%async_computation.8 | async-start | bytes 4915200 | tf_op jit(solution)/shard_map/all_gather | solution.py:1005
  105.3 25.0 %collective-permute-start.16 = (bf16[6,48,1792]{2,1,0:T(8,128)(2,1)S(1)}, bf16[6,48,1792]{2,1,0:T(8,128)(2,1)}, u32[]{:S(2)}, u32[]{:S(2)}) collective-permute-start(bf16[6,48,1792]{2,1,0:T(8,128)(2,1)S(1)} %pad_maximum_fusion.4), channel_id=1, source_target_pairs={{0,2},{2,0},{4,6},{6,4},{1,3},{3,1},{5,7},{7,5},{8,10},{10,8},{12,... | collective-permute-start | bytes 3096584 | tf_op jit(solution)/shard_map/ppermute | solution.py:27
  106.9 23.2 %collective-permute-start.15 = (bf16[6,48,1664]{2,1,0:T(8,128)(2,1)}, bf16[6,48,1664]{2,1,0:T(8,128)(2,1)S(1)}, u32[]{:S(2)}, u32[]{:S(2)}) collective-permute-start(bf16[6,48,1664]{2,1,0:T(8,128)(2,1)} %pad_maximum_fusion.6), channel_id=1, source_target_pairs={{0,4},{2,6},{4,0},{6,2},{1,5},{3,7},{5,1},{7,3},{8,12},{10,14},{12... | collective-permute-start | bytes 2875400 | tf_op jit(solution)/shard_map/ppermute | solution.py:27
  120.1 16.3 %collective-permute-start.14 = (f32[256,768]{1,0:T(8,128)}, f32[256,768]{1,0:T(8,128)S(1)}, u32[]{:S(2)}, u32[]{:S(2)}) collective-permute-start(f32[256,768]{1,0:T(8,128)} %get-tuple-element.173.a_ref), channel_id=1, source_target_pairs={{0,1},{1,0},{2,3},{3,2},{4,5},{5,4},{6,7},{7,6},{8,9},{9,8},{10,11... | collective-permute-start | bytes 2359304 | tf_op jit(solution)/shard_map/ppermute | solution.py:27
  147.1 220.8 %reduce-scatter.12.cloned.1.call-start = ((), (), s32[]{:S(2)}) async-start(), calls=%async_computation.11 | async-start | bytes 2211840
  162.9 16.0 %collective-permute-start.21 = (bf16[272,384]{1,0:T(8,128)(2,1)S(1)}, bf16[272,384]{1,0:T(8,128)(2,1)S(1)}, u32[]{:S(2)}, u32[]{:S(2)}) collective-permute-start(bf16[272,384]{1,0:T(8,128)(2,1)S(1)} %concatenate.130.refs_0_), channel_id=1, source_target_pairs={{0,16},{8,24},{16,0},{24,8},{1,17},{9,25},{17,1},{25,9},{2,18},{10... | collective-permute-start | bytes 626696 | tf_op jit(solution)/shard_map/ppermute | solution.py:32
  247.5 18.7 %collective-permute-start.38 = (bf16[256,384]{1,0:T(8,128)(2,1)}, bf16[256,384]{1,0:T(8,128)(2,1)S(1)}, u32[]{:S(2)}, u32[]{:S(2)}) collective-permute-start(bf16[256,384]{1,0:T(8,128)(2,1)} %get-tuple-element.208), channel_id=1, source_target_pairs={{0,16},{8,24},{16,0},{24,8},{1,17},{9,25},{17,1},{25,9},{2,18},{10... | collective-permute-start | bytes 589832 | tf_op jit(solution)/shard_map/ppermute | solution.py:32
  248.4 17.8 %collective-permute-start.39 = (bf16[256,384]{1,0:T(8,128)(2,1)}, bf16[256,384]{1,0:T(8,128)(2,1)S(1)}, u32[]{:S(2)}, u32[]{:S(2)}) collective-permute-start(bf16[256,384]{1,0:T(8,128)(2,1)} %get-tuple-element.209), channel_id=1, source_target_pairs={{0,8},{8,16},{16,24},{24,0},{1,9},{9,17},{17,25},{25,1},{2,10},{10... | collective-permute-start | bytes 589832 | tf_op jit(solution)/shard_map/ppermute | solution.py:32
  269.8 17.1 %collective-permute-start.35 = (bf16[256,384]{1,0:T(8,128)(2,1)S(1)}, bf16[256,384]{1,0:T(8,128)(2,1)S(1)}, u32[]{:S(2)}, u32[]{:S(2)}) collective-permute-start(bf16[256,384]{1,0:T(8,128)(2,1)S(1)} %copy-done.80), channel_id=1, source_target_pairs={{0,16},{8,24},{16,0},{24,8},{1,17},{9,25},{17,1},{25,9},{2,18},{10... | collective-permute-start | bytes 589832 | tf_op jit(solution)/shard_map/ppermute | solution.py:32
  273.8 121.7 %reduce-scatter.10.cloned.1.call-start = ((), (), s32[]{:S(2)}) async-start(), calls=%async_computation.10 | async-start | bytes 1474560
  287.1 34.4 %collective-permute-start.48 = (f32[256,768]{1,0:T(8,128)}, f32[256,768]{1,0:T(8,128)S(1)}, u32[]{:S(2)}, u32[]{:S(2)}) collective-permute-start(f32[256,768]{1,0:T(8,128)} %get-tuple-element.247.a_ref), channel_id=1, source_target_pairs={{0,1},{1,0},{2,3},{3,2},{4,5},{5,4},{6,7},{7,6},{8,9},{9,8},{10,11... | collective-permute-start | bytes 2359304 | tf_op jit(solution)/shard_map/ppermute | solution.py:27
  303.2 18.4 %collective-permute-start.47 = (bf16[512,384]{1,0:T(8,128)(2,1)S(1)}, bf16[512,384]{1,0:T(8,128)(2,1)S(1)}, u32[]{:S(2)}, u32[]{:S(2)}) collective-permute-start(bf16[512,384]{1,0:T(8,128)(2,1)S(1)} %get-tuple-element.380), channel_id=1, source_target_pairs={{0,6},{2,4},{4,2},{6,0},{1,7},{3,5},{5,3},{7,1},{8,14},{10,12},{12... | collective-permute-start | bytes 1179656 | tf_op jit(solution)/shard_map/ppermute | solution.py:27
  305.4 28.2 %collective-permute-start.67 = (bf16[1024,384]{1,0:T(8,128)(2,1)S(1)}, bf16[1024,384]{1,0:T(8,128)(2,1)S(1)}, u32[]{:S(2)}, u32[]{:S(2)}) collective-permute-start(bf16[1024,384]{1,0:T(8,128)(2,1)S(1)} %pad_maximum_fusion.8), channel_id=1, source_target_pairs={{0,1},{1,0},{2,3},{3,2},{4,5},{5,4},{6,7},{7,6},{8,9},{9,8},{10,11... | collective-permute-start | bytes 2359304 | tf_op jit(solution)/shard_map/ppermute | solution.py:27
  338.2 58.5 %reduce-scatter.8.cloned.1.call-start = ((), (), s32[]{:S(2)}) async-start(), calls=%async_computation.3 | async-start | bytes 737280 | tf_op jit(solution)/shard_map/reduce_scatter | solution.py:1067
  338.2 16.2 %collective-permute-start.49 = (bf16[768,384]{1,0:T(8,128)(2,1)S(1)}, bf16[768,384]{1,0:T(8,128)(2,1)S(1)}, u32[]{:S(2)}, u32[]{:S(2)}) collective-permute-start(bf16[768,384]{1,0:T(8,128)(2,1)S(1)} %copy-done.75), channel_id=1, source_target_pairs={{0,2},{2,0},{4,6},{6,4},{1,3},{3,1},{5,7},{7,5},{8,10},{10,8},{12,... | collective-permute-start | bytes 1769480 | tf_op jit(solution)/shard_map/ppermute | solution.py:27
  338.9 27.7 %collective-permute-start.50 = (bf16[768,384]{1,0:T(8,128)(2,1)S(1)}, bf16[768,384]{1,0:T(8,128)(2,1)S(1)}, u32[]{:S(2)}, u32[]{:S(2)}) collective-permute-start(bf16[768,384]{1,0:T(8,128)(2,1)S(1)} %copy-done.74), channel_id=1, source_target_pairs={{0,4},{2,6},{4,0},{6,2},{1,5},{3,7},{5,1},{7,3},{8,12},{10,14},{12... | collective-permute-start | bytes 1769480 | tf_op jit(solution)/shard_map/ppermute | solution.py:27
  339.6 27.1 %collective-permute-start.51 = (bf16[768,384]{1,0:T(8,128)(2,1)S(1)}, bf16[768,384]{1,0:T(8,128)(2,1)S(1)}, u32[]{:S(2)}, u32[]{:S(2)}) collective-permute-start(bf16[768,384]{1,0:T(8,128)(2,1)S(1)} %copy-done.73), channel_id=1, source_target_pairs={{0,6},{2,4},{4,2},{6,0},{1,7},{3,5},{5,3},{7,1},{8,14},{10,12},{12... | collective-permute-start | bytes 1769480 | tf_op jit(solution)/shard_map/ppermute | solution.py:27
  367.9 95.0 %all-gather.12.cloned.1.call-start = ((), (), s32[]{:S(2)}) async-start(), calls=%async_computation.4 | async-start | bytes 2211840 | tf_op jit(solution)/shard_map/all_gather | solution.py:1054
  368.7 99.0 %all-gather.22.cloned.1.call-start = ((), (), s32[]{:S(2)}) async-start(), calls=%async_computation.9 | async-start | bytes 2211840 | tf_op jit(solution)/shard_map/all_gather | solution.py:1080
  370.4 16.5 %collective-permute-start.54 = (bf16[256,768]{1,0:T(8,128)(2,1)S(1)}, bf16[256,768]{1,0:T(8,128)(2,1)S(1)}, u32[]{:S(2)}, u32[]{:S(2)}) collective-permute-start(bf16[256,768]{1,0:T(8,128)(2,1)S(1)} %copy-done.77), channel_id=1, source_target_pairs={{0,4},{2,6},{4,0},{6,2},{1,5},{3,7},{5,1},{7,3},{8,12},{10,14},{12... | collective-permute-start | bytes 1179656 | tf_op jit(solution)/shard_map/ppermute | solution.py:27
  371.0 17.3 %collective-permute-start.55 = (bf16[256,768]{1,0:T(8,128)(2,1)S(1)}, bf16[256,768]{1,0:T(8,128)(2,1)S(1)}, u32[]{:S(2)}, u32[]{:S(2)}) collective-permute-start(bf16[256,768]{1,0:T(8,128)(2,1)S(1)} %copy-done.76), channel_id=1, source_target_pairs={{0,6},{2,4},{4,2},{6,0},{1,7},{3,5},{5,3},{7,1},{8,14},{10,12},{12... | collective-permute-start | bytes 1179656 | tf_op jit(solution)/shard_map/ppermute | solution.py:27
  399.0 27.8 %collective-permute-start.60 = (f32[384,768]{1,0:T(8,128)S(1)}, f32[384,768]{1,0:T(8,128)}, u32[]{:S(2)}, u32[]{:S(2)}) collective-permute-start(f32[384,768]{1,0:T(8,128)S(1)} %copy-done.18), channel_id=1, source_target_pairs={{0,1},{1,0},{2,3},{3,2},{4,5},{5,4},{6,7},{7,6},{8,9},{9,8},{10,11... | collective-permute-start | bytes 3538952 | tf_op jit(solution)/shard_map/ppermute | solution.py:27
  418.4 18.5 %collective-permute-start.61 = (bf16[768,384]{1,0:T(8,128)(2,1)}, bf16[768,384]{1,0:T(8,128)(2,1)}, u32[]{:S(2)}, u32[]{:S(2)}) collective-permute-start(bf16[768,384]{1,0:T(8,128)(2,1)} %get-tuple-element.265), channel_id=1, source_target_pairs={{0,2},{2,0},{4,6},{6,4},{1,3},{3,1},{5,7},{7,5},{8,10},{10,8},{12,... | collective-permute-start | bytes 1769480 | tf_op jit(solution)/shard_map/ppermute | solution.py:27
  419.4 17.5 %collective-permute-start.62 = (bf16[768,384]{1,0:T(8,128)(2,1)}, bf16[768,384]{1,0:T(8,128)(2,1)}, u32[]{:S(2)}, u32[]{:S(2)}) collective-permute-start(bf16[768,384]{1,0:T(8,128)(2,1)} %get-tuple-element.266), channel_id=1, source_target_pairs={{0,4},{2,6},{4,0},{6,2},{1,5},{3,7},{5,1},{7,3},{8,12},{10,14},{12... | collective-permute-start | bytes 1769480 | tf_op jit(solution)/shard_map/ppermute | solution.py:27
  420.8 33.2 %collective-permute-start.63 = (bf16[768,384]{1,0:T(8,128)(2,1)}, bf16[768,384]{1,0:T(8,128)(2,1)}, u32[]{:S(2)}, u32[]{:S(2)}) collective-permute-start(bf16[768,384]{1,0:T(8,128)(2,1)} %get-tuple-element.267), channel_id=1, source_target_pairs={{0,6},{2,4},{4,2},{6,0},{1,7},{3,5},{5,3},{7,1},{8,14},{10,12},{12... | collective-permute-start | bytes 1769480 | tf_op jit(solution)/shard_map/ppermute | solution.py:27
  422.5 39.4 %collective-permute-start.59 = (f32[256,768]{1,0:T(8,128)}, f32[256,768]{1,0:T(8,128)S(1)}, u32[]{:S(2)}, u32[]{:S(2)}) collective-permute-start(f32[256,768]{1,0:T(8,128)} %get-tuple-element.270), channel_id=1, source_target_pairs={{0,1},{1,0},{2,3},{3,2},{4,5},{5,4},{6,7},{7,6},{8,9},{9,8},{10,11... | collective-permute-start | bytes 2359304 | tf_op jit(solution)/shard_map/ppermute | solution.py:27
  (131 other events, 1006.8 us)
Sparse Core Ops, SparseCore 0:
  10.3 31.1 all-gather.13
  43.7 32.4 all-gather.15
  105.0 26.5 all-gather.17
  147.3 49.5 all-gather.19
  273.9 32.2 reduce-scatter.11
  338.3 29.1 reduce-scatter.9
  369.8 20.6 reduce-scatter.7
  392.3 34.4 all-gather.11
  429.2 38.3 all-gather.21
where the time goes:
time: 504 us; the launch traced here: 497 us
  waiting for transfers between devices  200 us (40%)
  Pallas kernels  119 us (24%)
  starting transfers between devices  82.3 us (16%)
  local copies, waits for them, and re-layouts  49 us (10%)
  other arithmetic  23.2 us (5%)
  between operations  20.7 us (4%)
    ppermute x54, waiting for transfers between devices, swap(): return lax.ppermute(x, axis, [(i, i ^ bit) for i in range(size)])  126 us
    ppermute x54, starting transfers between devices, swap(): return lax.ppermute(x, axis, [(i, i ^ bit) for i in range(size)])  54.4 us
    ppermute x18, waiting for transfers between devices, turn(): return lax.ppermute(x, axis, [(i, (i + k) % size) for i in range(size)])  44.8 us
    ppermute x18, starting transfers between devices, turn(): return lax.ppermute(x, axis, [(i, (i + k) % size) for i in range(size)])  27.1 us
    all_gather x3, waiting for transfers between devices, gather_beside(): return lax.all_gather(x, Z)  23.8 us
    unnamed x170, local copies, waits for them, and re-layouts  19.4 us
    pallas_call x1, Pallas kernels, attend_back(): call(run, (whole((rows, width), F32), whole((rows, width), BF), whole((8,...  10.7 us
    pallas_call x1, Pallas kernels, attend(): call(run, (whole((rows, half), BF), whole((keys, 2 * half), BF), whole((8...  10.6 us
  transfers between devices with their start and end apart: 81, of which 46 were waited for; matrix products, arithmetic and copies ran while one was open for 10% of the time, Pallas kernels for 20%

commit v1 on v0

--- a/solution.py
+++ b/solution.py
@@ -125,51 +125,16 @@
 BOTH = ((1, 2), (2, 1))
 
 
-def sent_apart(products, b0, b1):
+def side_grads(products):
     rows, width = products[0][0].shape[1], products[0][1].shape[1]
-    arrays = []
-    places = []
-    for pair in products:
-        spots = []
-        for x in pair:
-            for i, y in enumerate(arrays):
-                if y is x:
-                    break
-            else:
-                i = len(arrays)
-                arrays.append(x)
-            spots.append(i)
-        places.append(spots)
-    count = len(arrays)
 
     def kernel(*refs):
-        outs = refs[count:]
-        c = lax.axis_index(C)
-        for j, (l, r) in enumerate(places):
-            part = dot(refs[l][...], refs[r][...], 0, 0).astype(BF)
-            if b1 is None:
-                for m in range(4):
-
-                    @pl.when(jnp.bitwise_xor(c, j) == m)
-                    def _():
-                        outs[m][...] = part
-            else:
-                slot = (j & b1) // b1
-                mine = jnp.bitwise_and(jnp.bitwise_xor(c, j), b0) == 0
-
-                @pl.when(mine)
-                def _():
-                    outs[0][slot] = part
-
-                @pl.when(jnp.logical_not(mine))
-                def _():
-                    outs[1][slot] = part
-
-    if b1 is None:
-        shapes = (whole((rows, width), BF),) * 4
-    else:
-        shapes = (whole((2, rows, width), BF),) * 2
-    return call(kernel, shapes, "grads")(*arrays)
+        for j in range(len(products)):
+            grad = dot(refs[2 * j][...], refs[2 * j + 1][...], 0, 0)
+            refs[-1][:, j * width : (j + 1) * width] = grad.astype(BF)
+
+    arrays = [x for pair in products for x in pair]
+    return call(kernel, whole((rows, width * len(products)), BF), "grads")(*arrays)
 
 
 def z_split(parts):
@@ -218,25 +183,31 @@
     return call(kernel, outs, name)(*parts)
 
 
-def early_join(copies):
-    _, rows, width = copies.shape
+def early_join(parts):
+    rows, width = parts[0].shape
     third = width // 3
 
-    def run(in_ref, up_ref, down_ref, tok_ref, char_ref, gru_ref):
-        for j in range(4):
-            at = slice(j * third, (j + 1) * third)
-            up_ref[:, at] = in_ref[j, :, :third].astype(F32)
-            down_ref[at] = in_ref[j, :, third : 2 * third].astype(F32).T
-        tok_ref[...] = in_ref[0, :, 2 * third :].astype(F32)
-        char_ref[...] = in_ref[1, :, 2 * third :].astype(F32).T
-        gru_ref[:, :third] = in_ref[2, :, 2 * third :].astype(F32)
-        gru_ref[:, third:] = in_ref[3, :, 2 * third :].astype(F32)
-
-    shapes = (
+    def store(j):
+        at = slice(j * third, (j + 1) * third)
+
+        def put(x, outs):
+            outs[0][:, at] = x[:, :third]
+            outs[1][at] = x[:, third : 2 * third].T
+            rest = x[:, 2 * third :]
+            if j == 0:
+                outs[2][...] = rest
+            elif j == 1:
+                outs[3][...] = rest.T
+            else:
+                outs[4][:, (j - 2) * third : (j - 1) * third] = rest
+
+        return put
+
+    outs = (
         whole((rows, 4 * third), F32), whole((4 * third, rows), F32), whole((rows, third), F32),
         whole((third, rows), F32), whole((rows, 2 * third), F32),
     )
-    return call(run, shapes, "early_join")(copies)
+    return by_context(parts, outs, [store(j) for j in range(4)], "early_join")
 
 
 def query_join(parts):
@@ -321,18 +292,27 @@
     part = rows // 2
 
     def run(*refs):
-        c_ref, w_ref, keep_ref, send_ref = refs[nz:]
+        c_ref, w_ref, keep_ref, send_ref, u_ref, rim_ref = refs[nz:]
         t = lax.axis_index(T)
+        for k in range(nz):
+            at = slice(k * rows, (k + 1) * rows)
+            u_ref[at, :half] = refs[k][:rows]
+            u_ref[at, half:] = c_ref[block_of(k, nz), :rows]
+            at = slice(16 * k, 16 * k + 16)
+            rim = refs[k][rows:]
+            rim_ref[at, :half] = rim
+            rim_ref[at, half:] = jnp.concatenate([rim[2:4], jnp.zeros((14, half), BF)])
+        before = dot(rim_ref[...], w_ref[0])
+        beyond = dot(rim_ref[...], w_ref[2])
+        taps = [dot(u_ref[...], w_ref[m]) for m in range(3)]
         at = lax.broadcasted_iota(jnp.int32, (rows, cols), 0)
         for k in range(nz):
-            j = block_of(k, nz)
-            u = jnp.concatenate([refs[k][:rows], c_ref[j, :rows]], axis=1)
-            rim = refs[k][rows:]
-            rim = jnp.concatenate([rim[:2], rim[2:4]], axis=1)
-            rim = jnp.concatenate([rim, jnp.zeros((14, 2 * half), BF)])
-            total = dot(u, w_ref[1])
-            total = total + jnp.where(at == 0, dot(rim, w_ref[0])[0:1], pltpu.roll(dot(u, w_ref[0]), 1, 0))
-            total = total + jnp.where(at == rows - 1, dot(rim, w_ref[2])[1:2], pltpu.roll(dot(u, w_ref[2]), rows - 1, 0))
+            here = slice(k * rows, (k + 1) * rows)
+            total = taps[1][here]
+            total = total + jnp.where(at == 0, before[16 * k : 16 * k + 1], pltpu.roll(taps[0][here], 1, 0))
+            total = total + jnp.where(
+                at == rows - 1, beyond[16 * k + 1 : 16 * k + 2], pltpu.roll(taps[2][here], rows - 1, 0)
+            )
 
             @pl.when(t == 0)
             def _():
@@ -345,7 +325,8 @@
                 send_ref[k] = total[:part]
 
     shape = whole((nz, part, cols), F32)
-    return call(run, (shape, shape), "conv")(*toks, chrs, kernel)
+    scratch = (pltpu.VMEM((nz * rows, 2 * half), BF), pltpu.VMEM((16 * nz, 2 * half), BF))
+    return call(run, (shape, shape), "conv", scratch)(*toks, chrs, kernel)
 
 
 def add_split(keep, came):
@@ -499,14 +480,11 @@
         m_ref, o_ref, w_ref = refs[:3]
         outs, (wide, whole_ref) = refs[3 : 3 + 2 * nz], refs[3 + 2 * nz :]
         spread_taps(m_ref, o_ref, wide, whole_ref)
-        for k in range(nz):
-            for side in range(2):
-                at = slice(side * half, (side + 1) * half)
-                x = sum(dot(wide[m, k], w_ref[m, at], 1, 1) for m in range(3)).astype(BF)
-                if side:
-                    outs[nz + k][...] = x
-                else:
-                    outs[k][...] = x
+        for side in range(2):
+            at = slice(side * half, (side + 1) * half)
+            x = sum(dot(wide[m].reshape(nz * rows, cols), w_ref[m, at], 1, 1) for m in range(3)).astype(BF)
+            for k in range(nz):
+                outs[side * nz + k][...] = x[k * rows : (k + 1) * rows]
 
     shapes = (whole((rows, half), BF),) * (2 * nz)
     outs = call(run, shapes, "conv_back", tap_scratch(mine))(mine, other, kernel)
@@ -1048,50 +1026,49 @@
         scans, ends_all, d_hidden, proj, bias, marks, states, (entries,), w_recur
     )
     d_chr_in = d_res_four + core_sum(part_chr)
-    sent = sent_apart(((second_low, dfa), (dfb_full, pooled_low), (chars_in, d_low), (chars_in, d_high)), 1, None)
-    chars_own, *chars_sent = sent
-
+    chars_grads = side_grads(((second_low, dfa), (dfb_full, pooled_low), (chars_in, d_low), (chars_in, d_high)))
+    chars_grads_z = lax.psum_scatter(chars_grads, Z, scatter_dimension=0, tiled=True)
     grad_kernel = lax.all_gather(grad_kernel, C)
 
-    pre_came = after(pre_came, chars_sent)
-    chars_came = [swap(x, C, m) for m, x in zip((1, 2, 3), chars_sent)]
     d_res_one, d_att, stats_one, dq, dkv_own, *dkv_sends = attend_back(
-        after(d_res_two, pre_came), part, swap(part, T, 1), n_one, inv_one, gains, w_mix_t, q, kv, lse, seg_keys, seg_row
+        after(d_res_two, chars_grads), part, swap(part, T, 1), n_one, inv_one, gains, w_mix_t, q, kv, lse, seg_keys, seg_row
     )
     came = [swap(x, C, m) for m, x in zip((1, 2, 3), dkv_sends)]
     ffn_all, pre_part = collected(d_ffn, pre_own, after(pre_came, dq))
     g_up = dot(first_all, pre_part, 0, 0).astype(BF)
     g_down = dot(ffn_all, act_part, 0, 0).astype(BF)
     ffn_piece = lax.psum_scatter(jnp.concatenate([g_up, g_down], axis=1), Z, scatter_dimension=0, tiled=True)
-    chars_came = after(chars_came, dq)
-    chars_piece = lax.psum_scatter(summed(chars_own, chars_came), Z, scatter_dimension=0, tiled=True)
-
     counted = jnp.full((1, width), jnp.sum(valid_tok))
     packed = jnp.concatenate([stats[:5], counted, stats_bias[:2], stats_one[:2], stats_two[:2]])
-    packed = after(packed, chars_came)
-    packed = packed + swap(packed, C, 1)
-
-    *sent, part = query_grads(tokens_in, d_att, mixed_low, dq, dkv_own, came, w_query)
-    query_own, *query_sent = sent
-    query_came = [swap(x, C, m) for m, x in zip((1, 2, 3), query_sent)]
-    d_tok_in = d_res_one + core_sum(part)
-    query_blocks = z_split([query_own] + query_came)
-    query_turned = turned(query_blocks)
-    copies = lax.all_gather(jnp.concatenate(after([ffn_piece, chars_piece], query_sent), axis=1), C)
-    copies = after(copies, query_blocks)
-    grad_kernel = after(grad_kernel, query_blocks).reshape(2, 2, 3, half // 2, cols).astype(F32)
-    grad_kernel = grad_kernel.transpose(2, 0, 1, 3, 4)
-    g_up, g_down, g_tok, g_char, g_gru = early_join(copies)
-    query_turned = after(query_turned, g_up)
-    query_piece = summed(query_blocks[0], query_turned)
-    g_out, g_query = query_join([query_piece] + swapped(query_piece))
-
-    packed = after(packed, query_sent)
-    packed = packed + swap(packed, C, 2)
     bit = 1
     while bit < nz:
         packed = packed + swap(packed, Z, bit)
         bit *= 2
+
+    *sent, part = query_grads(tokens_in, d_att, mixed_low, dq, dkv_own, after(came, packed), w_query)
+    query_own, *query_sent = sent
+    query_came = [swap(x, C, m) for m, x in zip((1, 2, 3), query_sent)]
+    d_tok_in = d_res_one + core_sum(part)
+    quarters = after(chars_grads_z, query_sent)
+    quarters = [own_part(quarters, 4, jnp.bitwise_xor(c, m), 1) for m in range(4)]
+    chars_came = [swap(quarters[m], C, m) for m in (1, 2, 3)]
+    query_came = after(query_came, chars_came)
+    query_blocks = z_split([query_own] + query_came)
+    query_turned = turned(query_blocks)
+    ffn_piece = after(ffn_piece, query_came)
+    chars_piece = summed(quarters[0], chars_came)
+    early = jnp.concatenate([ffn_piece, chars_piece], axis=1)
+    early_copies = swapped(early)
+    query_piece = summed(query_blocks[0], query_turned)
+    query_copies = swapped(query_piece)
+    g_up, g_down, g_tok, g_char, g_gru = early_join([early] + after(early_copies, query_piece))
+    grad_kernel = after(grad_kernel, g_up).reshape(2, 2, 3, half // 2, cols).astype(F32)
+    grad_kernel = grad_kernel.transpose(2, 0, 1, 3, 4)
+    g_out, g_query = query_join([query_piece] + after(query_copies, g_up))
+
+    packed = after(packed, query_came)
+    for bit in (1, 2):
+        packed = packed + swap(packed, C, bit)
     loss = jnp.sum(packed[4]) / packed[5, 0]
     gain_total = jnp.stack([packed[8], packed[10], packed[0], packed[1]])[None]
     shift_total = jnp.stack([packed[9], packed[11], packed[2], packed[3]])[None]

time: 504 us -> 492 us (0.976)
  waiting for transfers between devices: 200 us -> 174 us
  other arithmetic: 23.2 us -> 29.2 us
    ppermute x54 -> x57, waiting for transfers between devices: 126 us -> 93.6 us  [swap(): return lax.ppermute(x, axis, [(i, i ^ bit) for i in range(size)])]
    ppermute x18, waiting for transfers between devices: 44.8 us -> 57 us  [turn(): return lax.ppermute(x, axis, [(i, (i + k) % size) for i in range(size)])]
    ppermute x54 -> x57, starting transfers between devices: 54.4 us -> 60.5 us  [swap(): return lax.ppermute(x, axis, [(i, i ^ bit) for i in range(size)])]
    pallas_call x3 -> x2, Pallas kernels: 16.9 us -> 11.2 us  [the longest x1 6.65 us: conv_main(): return call(run, (shape, shape), 'conv', scratch)(*toks, chrs, kernel)]
    unnamed x170 -> x157, local copies, waits for them, and re-layouts: 19.4 us -> 22.1 us
  transfers between devices with their start and end apart: 81 -> 83, of which waited for: 46 -> 48; matrix products, arithmetic and copies ran while one was open for 10% -> 11% of each run, Pallas kernels for 20% -> 22%
where the time goes in v1:
time: 492 us; the launch traced here: 484 us
  waiting for transfers between devices  174 us (35%)
  Pallas kernels  118 us (24%)
  starting transfers between devices  86.7 us (18%)
  local copies, waits for them, and re-layouts  53.3 us (11%)
  other arithmetic  29.2 us (6%)
  between operations  20.8 us (4%)
    ppermute x57, waiting for transfers between devices, swap(): return lax.ppermute(x, axis, [(i, i ^ bit) for i in range(size)])  93.6 us
    ppermute x57, starting transfers between devices, swap(): return lax.ppermute(x, axis, [(i, i ^ bit) for i in range(size)])  60.5 us
    ppermute x18, waiting for transfers between devices, turn(): return lax.ppermute(x, axis, [(i, (i + k) % size) for i in range(size)])  57 us
    ppermute x18, starting transfers between devices, turn(): return lax.ppermute(x, axis, [(i, (i + k) % size) for i in range(size)])  25.3 us
    all_gather x3, waiting for transfers between devices, gather_beside(): return lax.all_gather(x, Z)  23.8 us
    unnamed x157, local copies, waits for them, and re-layouts  22.1 us
    pallas_call x1, Pallas kernels, attend_back(): call(run, (whole((rows, width), F32), whole((rows, width), BF), whole((8,...  10.9 us
    pallas_call x1, Pallas kernels, attend(): call(run, (whole((rows, half), BF), whole((keys, 2 * half), BF), whole((8...  10.7 us
  transfers between devices with their start and end apart: 83, of which 48 were waited for; matrix products, arithmetic and copies ran while one was open for 11% of the time, Pallas kernels for 22%

profile of v1, /device:TPU:0, one launch (start us, length us, event | category | flops | bytes accessed | tf_op | source)
XLA Modules:
  0.0 484.5 jit_solution(12901823449983678180)
XLA Ops:
  19.1 4.8 collective-permute-done.1
  27.2 14.3 %all-gather.12.cloned.1.call-done = bf16[192,2816]{1,0:T(8,128)(2,1)} async-done(((bf16[48,2816]{1,0:T(8,128)(2,1)}), bf16[192,2816]{1,0:T(8,128)(2,1)}) %all-gather.12.cloned.1.call-update) | async-done | bytes 1081360 | tf_op jit(solution)/shard_map/all_gather | solution.py:261
  46.9 6.3 %collective-permute-done.4.refs_1_ = bf16[3,48,1280]{2,1,0:T(8,128)(2,1)S(1)} collective-permute-done((bf16[3,48,1280]{2,1,0:T(8,128)(2,1)S(1)}, bf16[3,48,1280]{2,1,0:T(8,128)(2,1)S(1)}, u32[]{:S(2)}, u32[]{:S(2)}) %collective-permute-start.4) | collective-permute-done | bytes 368672 | tf_op jit(solution)/shard_map/ppermute | solution.py:27
  66.7 9.5 %all-gather.14.cloned.1.call-done = bf16[192,3456]{1,0:T(8,128)(2,1)} async-done(((bf16[48,3456]{1,0:T(8,128)(2,1)}), bf16[192,3456]{1,0:T(8,128)(2,1)}) %all-gather.14.cloned.1.call-update) | async-done | bytes 1327120 | tf_op jit(solution)/shard_map/all_gather | solution.py:261
  82.0 4.5 assemble.2
  86.5 4.7 gru_open.1
  109.5 10.7 %attend.1 = (bf16[256,384]{1,0:T(8,128)(2,1)}, bf16[1024,768]{1,0:T(8,128)(2,1)}, f32[8,256]{1,0:T(8,128)}, bf16[256,384]{1,0:T(8,128)(2,1)}, f32[256,768]{1,0:T(8,128)}) custom-call(bf16[256,768]{1,0:T(8,128)(2,1)} %x_ref.3, bf16[3,256,768]{2,1,0:T(8,128)(2,1)} %pad_maximum_fusion.1.o_ref, bf16[768,1152]{1,0:T(8,128)(2,1)} %get-tuple-element.168.w_ref, ...), custom_call_target="tpu_custom_call" | custom-call | flops 1 | bytes 1 | tf_op jit(solution)/shard_map/attend/pallas_call | solution.py:701
  120.1 10.0 %collective-permute-done.15.refs_2_ = bf16[6,48,1664]{2,1,0:T(8,128)(2,1)S(1)} collective-permute-done((bf16[6,48,1664]{2,1,0:T(8,128)(2,1)}, bf16[6,48,1664]{2,1,0:T(8,128)(2,1)S(1)}, u32[]{:S(2)}, u32[]{:S(2)}) %collective-permute-start.15) | collective-permute-done | bytes 958496 | tf_op jit(solution)/shard_map/ppermute | solution.py:27
  131.1 5.3 %assemble.3 = (bf16[768,1536]{1,0:T(8,128)(2,1)}, bf16[768,384]{1,0:T(8,128)(2,1)}, bf16[768,1536]{1,0:T(8,128)(2,1)}) custom-call(bf16[3,48,1664]{2,1,0:T(8,128)(2,1)} %copy-done.4, bf16[3,48,1664]{2,1,0:T(8,128)(2,1)} %copy-done.10, bf16[6,48,1664]{2,1,0:T(8,128)(2,1)} %copy-done.19, bf16[3,48,1792]{2,1,0:T(8,128)(2,1)} %copy-done.3, ...), custom_call_target="tpu_custom_call" | custom-call | flops 1 | bytes 1 | tf_op jit(solution)/shard_map/assemble/pallas_call | solution.py:122
  137.3 6.7 %feed.1 = (f32[256,768]{1,0:T(8,128)}, f32[256,1]{1,0:T(8,128)}, bf16[256,768]{1,0:T(8,128)(2,1)}, f32[256,1536]{1,0:T(8,128)}, bf16[256,1536]{1,0:T(8,128)(2,1)}, /*index=5*/f32[256,768]{1,0:T(8,128)}) custom-call(bf16[256,768]{1,0:T(8,128)(2,1)} %x_ref.3, f32[256,768]{1,0:T(8,128)} %get-tuple-element.170.a_ref, f32[256,768]{1,0:T(8,128)} %copy-done.24, ...), custom_call_target="tpu_custom_call" | custom-call | flops 1 | bytes 1 | tf_op jit(solution)/shard_map/feed/pallas_call | solution.py:816
  166.9 5.2 %collective-permute-done.20.refs_1_ = bf16[272,384]{1,0:T(8,128)(2,1)S(1)} collective-permute-done((bf16[272,384]{1,0:T(8,128)(2,1)S(1)}, bf16[272,384]{1,0:T(8,128)(2,1)S(1)}, u32[]{:S(2)}, u32[]{:S(2)}) %collective-permute-start.20) | collective-permute-done | bytes 208928 | tf_op jit(solution)/shard_map/ppermute | solution.py:32
  172.2 6.8 %collective-permute-done.21.refs_2_ = bf16[272,384]{1,0:T(8,128)(2,1)S(1)} collective-permute-done((bf16[272,384]{1,0:T(8,128)(2,1)S(1)}, bf16[272,384]{1,0:T(8,128)(2,1)S(1)}, u32[]{:S(2)}, u32[]{:S(2)}) %collective-permute-start.21) | collective-permute-done | bytes 208928 | tf_op jit(solution)/shard_map/ppermute | solution.py:32
  179.7 6.7 %conv.1 = (f32[4,128,384]{2,1,0:T(8,128)}, f32[4,128,384]{2,1,0:T(8,128)}) custom-call(bf16[272,384]{1,0:T(8,128)(2,1)} %copy-done.11, bf16[272,384]{1,0:T(8,128)(2,1)} %copy-done.20, bf16[272,384]{1,0:T(8,128)(2,1)} %copy-done.21, bf16[272,384]{1,0:T(8,128)(2,1)} %copy-done.22, bf16[4,352,384]{2,1,0:T(8,128)(2,1)} %bitcast.98, bf16[3,768,384]{2,1,0:T(8,128)(2,1)} %bitcast.96), custom_call_target="tpu_custom_call" | custom-call | flops 1 | bytes 1 | tf_op jit(solution)/shard_map/conv/pallas_call | solution.py:329
  191.9 4.8 collective-permute-start.24
  200.2 6.9 %collective-permute-done.25.refs_2_ = bf16[128,384]{1,0:T(8,128)(2,1)S(1)} collective-permute-done((bf16[128,384]{1,0:T(8,128)(2,1)}, bf16[128,384]{1,0:T(8,128)(2,1)S(1)}, u32[]{:S(2)}, u32[]{:S(2)}) %collective-permute-start.25) | collective-permute-done | bytes 98336 | tf_op jit(solution)/shard_map/ppermute | solution.py:32
  212.2 5.6 %close.1 = (f32[256,768]{1,0:T(8,128)}, f32[384,768]{1,0:T(8,128)}, f32[256,768]{1,0:T(8,128)}, f32[384,768]{1,0:T(8,128)}, bf16[128,1536]{1,0:T(8,128)(2,1)}, /*index=5*/f32[8,768]{1,0:T(8,128)}) custom-call(f32[256,768]{1,0:T(8,128)} %get-tuple-element.180.s_ref, bf16[128,1536]{1,0:T(8,128)(2,1)} %side_by_side.1.ym_ref, bf16[128,1536]{1,0:T(8,128)(2,1)} %copy-done.42, ...), custom_call_target="tpu_custom_call" | custom-call | flops 1 | bytes 1 | tf_op jit(solution)/shard_map/close/pallas_call | solution.py:439
  238.2 6.0 %conv_grads.1 = bf16[4,3,192,384]{3,2,1,0:T(8,128)(2,1)} custom-call(bf16[272,384]{1,0:T(8,128)(2,1)} %copy-done.11, bf16[272,384]{1,0:T(8,128)(2,1)} %copy-done.20, bf16[272,384]{1,0:T(8,128)(2,1)} %copy-done.21, bf16[272,384]{1,0:T(8,128)(2,1)} %copy-done.22, bf16[4,352,384]{2,1,0:T(8,128)(2,1)} %bitcast.99, bf16[4,144,384]{2,1,0:T(8,128)(2,1)} %copy-done.5, ...), custom_call_target="tpu_custom_call" | custom-call | flops 1 | bytes 1 | tf_op jit(solution)/shard_map/conv_grads/pallas_call | solution.py:512
  244.5 5.9 %conv_back.1 = (bf16[256,384]{1,0:T(8,128)(2,1)}, bf16[256,384]{1,0:T(8,128)(2,1)}, bf16[256,384]{1,0:T(8,128)(2,1)}, bf16[256,384]{1,0:T(8,128)(2,1)}, bf16[256...) custom-call(bf16[4,144,384]{2,1,0:T(8,128)(2,1)} %copy-done.5, ...), custom_call_target="tpu_custom_call" | custom-call | flops 1 | bytes 1 | tf_op jit(solution)/shard_map/conv_back/pallas_call | solution.py:490
  253.8 4.7 collective-permute-done.37.refs_1_
  258.5 13.0 %collective-permute-done.38.refs_2_ = bf16[256,384]{1,0:T(8,128)(2,1)S(1)} collective-permute-done((bf16[256,384]{1,0:T(8,128)(2,1)}, bf16[256,384]{1,0:T(8,128)(2,1)S(1)}, u32[]{:S(2)}, u32[]{:S(2)}) %collective-permute-start.38) | collective-permute-done | bytes 196640 | tf_op jit(solution)/shard_map/ppermute | solution.py:32
  279.9 7.2 %feed_back.1 = (f32[256,768]{1,0:T(8,128)}, bf16[256,768]{1,0:T(8,128)(2,1)}, bf16[256,1536]{1,0:T(8,128)(2,1)}, f32[256,768]{1,0:T(8,128)}, f32[8,768]{1,0:T(8,128)}) custom-call(f32[256,768]{1,0:T(8,128)} %get-tuple-element.202.d_ref, f32[256,768]{1,0:T(8,128)} %get-tuple-element.210.a_ref, f32[256,768]{1,0:T(8,128)} %copy-done.25, ...), custom_call_target="tpu_custom_call" | custom-call | flops 1 | bytes 1 | tf_op jit(solution)/shard_map/feed_back/pallas_call | solution.py:888
  287.1 5.3 %collective-permute-done.35 = bf16[256,384]{1,0:T(8,128)(2,1)S(1)} collective-permute-done((bf16[256,384]{1,0:T(8,128)(2,1)}, bf16[256,384]{1,0:T(8,128)(2,1)S(1)}, u32[]{:S(2)}, u32[]{:S(2)}) %collective-permute-start.35) | collective-permute-done | bytes 196640 | tf_op jit(solution)/shard_map/ppermute | solution.py:32
  294.8 4.5 gru_back_open.1
  306.7 5.2 %gru_back_close.1 = (bf16[384,384]{1,0:T(8,128)(2,1)}, bf16[384,384]{1,0:T(8,128)(2,1)}, f32[8,768]{1,0:T(8,128)}, f32[384,768]{1,0:T(8,128)}) custom-call(f32[384,192]{1,0:T(8,128)} %get-tuple-element.219.cd, f32[384,192]{1,0:T(8,128)} %get-tuple-element.220.md, f32[384,192]{1,0:T(8,128)} %get-tuple-element.221.cu, f32[384,192]{1,0:T(8,128)} %get-tuple-element.222.mu, ...), custom_call_target="tpu_custom_call" | custom-call | flops 1 | bytes 1 | tf_op jit(solution)/shard_map/gru_back_close/pallas_call | solution.py:668
  311.9 4.6 grads.1
  324.1 10.9 %attend_back.1 = (f32[256,768]{1,0:T(8,128)}, bf16[256,768]{1,0:T(8,128)(2,1)}, f32[8,768]{1,0:T(8,128)}, bf16[256,384]{1,0:T(8,128)(2,1)}, f32[256,768]{1,0:T(8...) custom-call(f32[256,768]{1,0:T(8,128)} %get-tuple-element.235.d_ref, ...), custom_call_target="tpu_custom_call" | custom-call | flops 1 | bytes 1 | tf_op jit(solution)/shard_map/attend_back/pallas_call | solution.py:753
  355.6 4.3 collective-permute-start.46
  370.9 6.8 %query_grads.1 = (bf16[768,384]{1,0:T(8,128)(2,1)}, bf16[768,384]{1,0:T(8,128)(2,1)}, bf16[768,384]{1,0:T(8,128)(2,1)}, bf16[768,384]{1,0:T(8,128)(2,1)}, f32[256,768]{1,0:T(8,128)}) custom-call(bf16[256,768]{1,0:T(8,128)(2,1)} %x_ref.3, bf16[256,768]{1,0:T(8,128)(2,1)} %get-tuple-element.243.da_ref, bf16[256,384]{1,0:T(8,128)(2,1)} %get-tuple-element.244.att_ref, ...), custom_call_target="tpu_custom_call" | custom-call | flops 1 | bytes 1 | tf_op jit(solution)/shard_map/query_grads/pallas_call | solution.py:784
  385.2 9.1 %collective-permute-done.51.refs_1_ = bf16[768,384]{1,0:T(8,128)(2,1)} collective-permute-done((bf16[768,384]{1,0:T(8,128)(2,1)}, bf16[768,384]{1,0:T(8,128)(2,1)}, u32[]{:S(2)}, u32[]{:S(2)}) %collective-permute-start.51) | collective-permute-done | bytes 589856 | tf_op jit(solution)/shard_map/ppermute | solution.py:27
  399.8 7.9 %collective-permute-done.52.refs_2_ = bf16[768,384]{1,0:T(8,128)(2,1)} collective-permute-done((bf16[768,384]{1,0:T(8,128)(2,1)}, bf16[768,384]{1,0:T(8,128)(2,1)}, u32[]{:S(2)}, u32[]{:S(2)}) %collective-permute-start.52) | collective-permute-done | bytes 589856 | tf_op jit(solution)/shard_map/ppermute | solution.py:27
  410.6 4.8 collective-permute-done.55
  448.1 8.4 %collective-permute-done.73.refs_2_ = bf16[192,1152]{1,0:T(8,128)(2,1)S(1)} collective-permute-done((bf16[192,1152]{1,0:T(8,128)(2,1)S(1)}, bf16[192,1152]{1,0:T(8,128)(2,1)S(1)}, u32[]{:S(2)}, u32[]{:S(2)}) %collective-permute-start.73) | collective-permute-done | bytes 442400 | tf_op jit(solution)/shard_map/ppermute | solution.py:27
  (441 shorter events, 242.7 us)
Async XLA Ops:
  7.2 34.3 %all-gather.12.cloned.1.call-start = ((), (), s32[]{:S(2)}) async-start(), calls=%async_computation.6 | async-start | bytes 1351680 | tf_op jit(solution)/shard_map/all_gather | solution.py:261
  10.2 66.0 %all-gather.14.cloned.1.call-start = ((), (), s32[]{:S(2)}) async-start(), calls=%async_computation.7 | async-start | bytes 1658880 | tf_op jit(solution)/shard_map/all_gather | solution.py:261
  24.8 111.5 %all-gather.16.cloned.1.call-start = ((), (), s32[]{:S(2)}) async-start(), calls=%async_computation.8 | async-start | bytes 1351680 | tf_op jit(solution)/shard_map/all_gather | solution.py:261
  54.2 22.0 %collective-permute-start.5 = (bf16[6,48,1280]{2,1,0:T(8,128)(2,1)}, bf16[6,48,1280]{2,1,0:T(8,128)(2,1)S(1)}, u32[]{:S(2)}, u32[]{:S(2)}) collective-permute-start(bf16[6,48,1280]{2,1,0:T(8,128)(2,1)} %pad_maximum_fusion.9), channel_id=1, source_target_pairs={{0,4},{2,6},{4,0},{6,2},{1,5},{3,7},{5,1},{7,3},{8,12},{10,14},{12... | collective-permute-start | bytes 2211848 | tf_op jit(solution)/shard_map/ppermute | solution.py:27
  55.8 20.4 %collective-permute-start.7 = (bf16[6,48,1408]{2,1,0:T(8,128)(2,1)S(1)}, bf16[6,48,1408]{2,1,0:T(8,128)(2,1)S(1)}, u32[]{:S(2)}, u32[]{:S(2)}) collective-permute-start(bf16[6,48,1408]{2,1,0:T(8,128)(2,1)S(1)} %pad_maximum_fusion.7), channel_id=1, source_target_pairs={{0,2},{2,0},{4,6},{6,4},{1,3},{3,1},{5,7},{7,5},{8,10},{10,8},{12,... | collective-permute-start | bytes 2433032 | tf_op jit(solution)/shard_map/ppermute | solution.py:27
  104.9 139.6 %all-gather.18.cloned.1.call-start = ((), (), s32[]{:S(2)}) async-start(), calls=%async_computation.9 | async-start | bytes 4915200 | tf_op jit(solution)/shard_map/all_gather | solution.py:983
  105.3 25.0 %collective-permute-start.16 = (bf16[6,48,1792]{2,1,0:T(8,128)(2,1)S(1)}, bf16[6,48,1792]{2,1,0:T(8,128)(2,1)}, u32[]{:S(2)}, u32[]{:S(2)}) collective-permute-start(bf16[6,48,1792]{2,1,0:T(8,128)(2,1)S(1)} %pad_maximum_fusion.4), channel_id=1, source_target_pairs={{0,2},{2,0},{4,6},{6,4},{1,3},{3,1},{5,7},{7,5},{8,10},{10,8},{12,... | collective-permute-start | bytes 3096584 | tf_op jit(solution)/shard_map/ppermute | solution.py:27
  106.9 23.2 %collective-permute-start.15 = (bf16[6,48,1664]{2,1,0:T(8,128)(2,1)}, bf16[6,48,1664]{2,1,0:T(8,128)(2,1)S(1)}, u32[]{:S(2)}, u32[]{:S(2)}) collective-permute-start(bf16[6,48,1664]{2,1,0:T(8,128)(2,1)} %pad_maximum_fusion.6), channel_id=1, source_target_pairs={{0,4},{2,6},{4,0},{6,2},{1,5},{3,7},{5,1},{7,3},{8,12},{10,14},{12... | collective-permute-start | bytes 2875400 | tf_op jit(solution)/shard_map/ppermute | solution.py:27
  147.2 230.5 %reduce-scatter.10.cloned.1.call-start = ((), (), s32[]{:S(2)}) async-start(), calls=%async_computation.10 | async-start | bytes 2211840
  244.3 138.3 %reduce-scatter.6.cloned.1.call-start = ((), (), s32[]{:S(2)}) async-start(), calls=%async_computation.3 | async-start | bytes 2949120 | tf_op jit(solution)/shard_map/reduce_scatter | solution.py:1030
  252.9 18.7 %collective-permute-start.38 = (bf16[256,384]{1,0:T(8,128)(2,1)}, bf16[256,384]{1,0:T(8,128)(2,1)S(1)}, u32[]{:S(2)}, u32[]{:S(2)}) collective-permute-start(bf16[256,384]{1,0:T(8,128)(2,1)} %get-tuple-element.205), channel_id=1, source_target_pairs={{0,16},{8,24},{16,0},{24,8},{1,17},{9,25},{17,1},{25,9},{2,18},{10... | collective-permute-start | bytes 589832 | tf_op jit(solution)/shard_map/ppermute | solution.py:32
  253.8 17.8 %collective-permute-start.39 = (bf16[256,384]{1,0:T(8,128)(2,1)}, bf16[256,384]{1,0:T(8,128)(2,1)S(1)}, u32[]{:S(2)}, u32[]{:S(2)}) collective-permute-start(bf16[256,384]{1,0:T(8,128)(2,1)} %get-tuple-element.206), channel_id=1, source_target_pairs={{0,8},{8,16},{16,24},{24,0},{1,9},{9,17},{17,25},{25,1},{2,10},{10... | collective-permute-start | bytes 589832 | tf_op jit(solution)/shard_map/ppermute | solution.py:32
  316.5 104.2 %reduce-scatter.8.cloned.1.call-start = ((), (), s32[]{:S(2)}) async-start(), calls=%async_computation.4 | async-start | bytes 1474560 | tf_op jit(solution)/shard_map/reduce_scatter | solution.py:1040
  319.4 17.8 %collective-permute-start.69 = (bf16[512,384]{1,0:T(8,128)(2,1)S(1)}, bf16[512,384]{1,0:T(8,128)(2,1)S(1)}, u32[]{:S(2)}, u32[]{:S(2)}) collective-permute-start(bf16[512,384]{1,0:T(8,128)(2,1)S(1)} %get-tuple-element.378), channel_id=1, source_target_pairs={{0,4},{2,6},{4,0},{6,2},{1,5},{3,7},{5,1},{7,3},{8,12},{10,14},{12... | collective-permute-start | bytes 1179656 | tf_op jit(solution)/shard_map/ppermute | solution.py:27
  320.2 18.6 %collective-permute-start.70 = (bf16[512,384]{1,0:T(8,128)(2,1)S(1)}, bf16[512,384]{1,0:T(8,128)(2,1)S(1)}, u32[]{:S(2)}, u32[]{:S(2)}) collective-permute-start(bf16[512,384]{1,0:T(8,128)(2,1)S(1)} %get-tuple-element.377), channel_id=1, source_target_pairs={{0,6},{2,4},{4,2},{6,0},{1,7},{3,5},{5,3},{7,1},{8,14},{10,12},{12... | collective-permute-start | bytes 1179656 | tf_op jit(solution)/shard_map/ppermute | solution.py:27
  343.8 118.3 %all-gather.10.cloned.1.call-start = ((), (), s32[]{:S(2)}) async-start(), calls=%async_computation.5 | async-start | bytes 2211840 | tf_op jit(solution)/shard_map/all_gather | solution.py:1031
  344.3 37.0 %collective-permute-start.60 = (f32[384,768]{1,0:T(8,128)S(1)}, f32[384,768]{1,0:T(8,128)S(1)}, u32[]{:S(2)}, u32[]{:S(2)}) collective-permute-start(f32[384,768]{1,0:T(8,128)S(1)} %copy-done.18), channel_id=1, source_target_pairs={{0,1},{1,0},{2,3},{3,2},{4,5},{5,4},{6,7},{7,6},{8,9},{9,8},{10,11... | collective-permute-start | bytes 3538952 | tf_op jit(solution)/shard_map/ppermute | solution.py:27
  344.8 25.1 %collective-permute-start.48 = (bf16[256,768]{1,0:T(8,128)(2,1)}, bf16[256,768]{1,0:T(8,128)(2,1)S(1)}, u32[]{:S(2)}, u32[]{:S(2)}) collective-permute-start(bf16[256,768]{1,0:T(8,128)(2,1)} %get-tuple-element.247), channel_id=1, source_target_pairs={{0,2},{2,0},{4,6},{6,4},{1,3},{3,1},{5,7},{7,5},{8,10},{10,8},{12,... | collective-permute-start | bytes 1179656 | tf_op jit(solution)/shard_map/ppermute | solution.py:27
  345.6 24.3 %collective-permute-start.49 = (bf16[256,768]{1,0:T(8,128)(2,1)}, bf16[256,768]{1,0:T(8,128)(2,1)S(1)}, u32[]{:S(2)}, u32[]{:S(2)}) collective-permute-start(bf16[256,768]{1,0:T(8,128)(2,1)} %get-tuple-element.248), channel_id=1, source_target_pairs={{0,4},{2,6},{4,0},{6,2},{1,5},{3,7},{5,1},{7,3},{8,12},{10,14},{12... | collective-permute-start | bytes 1179656 | tf_op jit(solution)/shard_map/ppermute | solution.py:27
  347.1 22.9 %collective-permute-start.50 = (bf16[256,768]{1,0:T(8,128)(2,1)}, bf16[256,768]{1,0:T(8,128)(2,1)S(1)}, u32[]{:S(2)}, u32[]{:S(2)}) collective-permute-start(bf16[256,768]{1,0:T(8,128)(2,1)} %get-tuple-element.249), channel_id=1, source_target_pairs={{0,6},{2,4},{4,2},{6,0},{1,7},{3,5},{5,3},{7,1},{8,14},{10,12},{12... | collective-permute-start | bytes 1179656 | tf_op jit(solution)/shard_map/ppermute | solution.py:27
  377.7 18.0 %collective-permute-start.59 = (f32[256,768]{1,0:T(8,128)}, f32[256,768]{1,0:T(8,128)}, u32[]{:S(2)}, u32[]{:S(2)}) collective-permute-start(f32[256,768]{1,0:T(8,128)} %get-tuple-element.262), channel_id=1, source_target_pairs={{0,1},{1,0},{2,3},{3,2},{4,5},{5,4},{6,7},{7,6},{8,9},{9,8},{10,11... | collective-permute-start | bytes 2359304 | tf_op jit(solution)/shard_map/ppermute | solution.py:27
  379.3 28.4 %collective-permute-start.52 = (bf16[768,384]{1,0:T(8,128)(2,1)}, bf16[768,384]{1,0:T(8,128)(2,1)}, u32[]{:S(2)}, u32[]{:S(2)}) collective-permute-start(bf16[768,384]{1,0:T(8,128)(2,1)} %get-tuple-element.254), channel_id=1, source_target_pairs={{0,4},{2,6},{4,0},{6,2},{1,5},{3,7},{5,1},{7,3},{8,12},{10,14},{12... | collective-permute-start | bytes 1769480 | tf_op jit(solution)/shard_map/ppermute | solution.py:27
  380.8 27.1 %collective-permute-start.53 = (bf16[768,384]{1,0:T(8,128)(2,1)}, bf16[768,384]{1,0:T(8,128)(2,1)}, u32[]{:S(2)}, u32[]{:S(2)}) collective-permute-start(bf16[768,384]{1,0:T(8,128)(2,1)} %get-tuple-element.255), channel_id=1, source_target_pairs={{0,6},{2,4},{4,2},{6,0},{1,7},{3,5},{5,3},{7,1},{8,14},{10,12},{12... | collective-permute-start | bytes 1769480 | tf_op jit(solution)/shard_map/ppermute | solution.py:27
  383.6 26.9 %collective-permute-start.54 = (bf16[192,384]{1,0:T(8,128)(2,1)S(1)}, bf16[192,384]{1,0:T(8,128)(2,1)S(1)}, u32[]{:S(2)}, u32[]{:S(2)}) collective-permute-start(bf16[192,384]{1,0:T(8,128)(2,1)S(1)} %get-tuple-element.362), channel_id=1, source_target_pairs={{0,2},{2,0},{4,6},{6,4},{1,3},{3,1},{5,7},{7,5},{8,10},{10,8},{12,... | collective-permute-start | bytes 442376 | tf_op jit(solution)/shard_map/ppermute | solution.py:27
  394.3 21.1 %collective-permute-start.55 = (bf16[192,384]{1,0:T(8,128)(2,1)S(1)}, bf16[192,384]{1,0:T(8,128)(2,1)S(1)}, u32[]{:S(2)}, u32[]{:S(2)}) collective-permute-start(bf16[192,384]{1,0:T(8,128)(2,1)S(1)} %get-tuple-element.361), channel_id=1, source_target_pairs={{0,4},{2,6},{4,0},{6,2},{1,5},{3,7},{5,1},{7,3},{8,12},{10,14},{12... | collective-permute-start | bytes 442376 | tf_op jit(solution)/shard_map/ppermute | solution.py:27
  395.7 21.5 %collective-permute-start.56 = (bf16[192,384]{1,0:T(8,128)(2,1)S(1)}, bf16[192,384]{1,0:T(8,128)(2,1)S(1)}, u32[]{:S(2)}, u32[]{:S(2)}) collective-permute-start(bf16[192,384]{1,0:T(8,128)(2,1)S(1)} %get-tuple-element.360), channel_id=1, source_target_pairs={{0,6},{2,4},{4,2},{6,0},{1,7},{3,5},{5,3},{7,1},{8,14},{10,12},{12... | collective-permute-start | bytes 442376 | tf_op jit(solution)/shard_map/ppermute | solution.py:27
  423.6 23.8 %collective-permute-start.72 = (bf16[192,1152]{1,0:T(8,128)(2,1)S(1)}, bf16[192,1152]{1,0:T(8,128)(2,1)S(1)}, u32[]{:S(2)}, u32[]{:S(2)}) collective-permute-start(bf16[192,1152]{1,0:T(8,128)(2,1)S(1)} %pad_maximum_fusion.19.refs_0_), channel_id=1, source_target_pairs={{0,2},{2,0},{4,6},{6,4},{1,3},{3,1},{5,7},{7,5},{8,10},{10,8},{12,... | collective-permute-start | bytes 1327112 | tf_op jit(solution)/shard_map/ppermute | solution.py:27
  425.7 30.8 %collective-permute-start.73 = (bf16[192,1152]{1,0:T(8,128)(2,1)S(1)}, bf16[192,1152]{1,0:T(8,128)(2,1)S(1)}, u32[]{:S(2)}, u32[]{:S(2)}) collective-permute-start(bf16[192,1152]{1,0:T(8,128)(2,1)S(1)} %pad_maximum_fusion.19.refs_0_), channel_id=1, source_target_pairs={{0,4},{2,6},{4,0},{6,2},{1,5},{3,7},{5,1},{7,3},{8,12},{10,14},{12... | collective-permute-start | bytes 1327112 | tf_op jit(solution)/shard_map/ppermute | solution.py:27
  427.0 29.5 %collective-permute-start.74 = (bf16[192,1152]{1,0:T(8,128)(2,1)S(1)}, bf16[192,1152]{1,0:T(8,128)(2,1)S(1)}, u32[]{:S(2)}, u32[]{:S(2)}) collective-permute-start(bf16[192,1152]{1,0:T(8,128)(2,1)S(1)} %pad_maximum_fusion.19.refs_0_), channel_id=1, source_target_pairs={{0,6},{2,4},{4,2},{6,0},{1,7},{3,5},{5,3},{7,1},{8,14},{10,12},{12... | collective-permute-start | bytes 1327112 | tf_op jit(solution)/shard_map/ppermute | solution.py:27
  444.6 21.4 %collective-permute-start.64 = (bf16[192,384]{1,0:T(8,128)(2,1)S(1)}, bf16[192,384]{1,0:T(8,128)(2,1)S(1)}, u32[]{:S(2)}, u32[]{:S(2)}) collective-permute-start(bf16[192,384]{1,0:T(8,128)(2,1)S(1)} %add_convert_fusion.3.refs_0_), channel_id=1, source_target_pairs={{0,2},{2,0},{4,6},{6,4},{1,3},{3,1},{5,7},{7,5},{8,10},{10,8},{12,... | collective-permute-start | bytes 442376 | tf_op jit(solution)/shard_map/ppermute | solution.py:27
  446.1 19.9 %collective-permute-start.65 = (bf16[192,384]{1,0:T(8,128)(2,1)S(1)}, bf16[192,384]{1,0:T(8,128)(2,1)S(1)}, u32[]{:S(2)}, u32[]{:S(2)}) collective-permute-start(bf16[192,384]{1,0:T(8,128)(2,1)S(1)} %add_convert_fusion.3.refs_0_), channel_id=1, source_target_pairs={{0,4},{2,6},{4,0},{6,2},{1,5},{3,7},{5,1},{7,3},{8,12},{10,14},{12... | collective-permute-start | bytes 442376 | tf_op jit(solution)/shard_map/ppermute | solution.py:27
  447.4 18.5 %collective-permute-start.66 = (bf16[192,384]{1,0:T(8,128)(2,1)S(1)}, bf16[192,384]{1,0:T(8,128)(2,1)S(1)}, u32[]{:S(2)}, u32[]{:S(2)}) collective-permute-start(bf16[192,384]{1,0:T(8,128)(2,1)S(1)} %add_convert_fusion.3.refs_0_), channel_id=1, source_target_pairs={{0,6},{2,4},{4,2},{6,0},{1,7},{3,5},{5,3},{7,1},{8,14},{10,12},{12... | collective-permute-start | bytes 442376 | tf_op jit(solution)/shard_map/ppermute | solution.py:27
  (127 other events, 875.9 us)
Sparse Core Ops, SparseCore 0:
  10.3 31.1 all-gather.11
  43.7 32.4 all-gather.13
  105.0 26.5 all-gather.15
  147.3 49.5 all-gather.17
  244.4 31.6 reduce-scatter.9
  316.6 50.4 reduce-scatter.5
  370.0 28.6 reduce-scatter.7
  400.5 45.3 all-gather.9

commit v2 on v1

--- a/solution.py
+++ b/solution.py
@@ -1058,7 +1058,7 @@
     ffn_piece = after(ffn_piece, query_came)
     chars_piece = summed(quarters[0], chars_came)
     early = jnp.concatenate([ffn_piece, chars_piece], axis=1)
-    early_copies = swapped(early)
+    early_copies = swapped(after(early, query_blocks))
     query_piece = summed(query_blocks[0], query_turned)
     query_copies = swapped(query_piece)
     g_up, g_down, g_tok, g_char, g_gru = early_join([early] + after(early_copies, query_piece))

time: 492 us -> 491 us (level)
  transfers between devices with their start and end apart: 83 -> 83, of which waited for: 48 -> 47; matrix products, arithmetic and copies ran while one was open for 11% -> 11% of each run, Pallas kernels for 22% -> 22%
where the time goes in v2:
time: 491 us; the launch traced here: 483 us
  waiting for transfers between devices  173 us (35%)
  Pallas kernels  118 us (24%)
  starting transfers between devices  87.5 us (18%)
  local copies, waits for them, and re-layouts  52.6 us (11%)
  other arithmetic  29.2 us (6%)
  between operations  20.8 us (4%)
    ppermute x57, waiting for transfers between devices, swap(): return lax.ppermute(x, axis, [(i, i ^ bit) for i in range(size)])  92.8 us
    ppermute x57, starting transfers between devices, swap(): return lax.ppermute(x, axis, [(i, i ^ bit) for i in range(size)])  60.3 us
    ppermute x18, waiting for transfers between devices, turn(): return lax.ppermute(x, axis, [(i, (i + k) % size) for i in range(size)])  56.1 us
    ppermute x18, starting transfers between devices, turn(): return lax.ppermute(x, axis, [(i, (i + k) % size) for i in range(size)])  26.3 us
    all_gather x3, waiting for transfers between devices, gather_beside(): return lax.all_gather(x, Z)  23.8 us
    unnamed x157, local copies, waits for them, and re-layouts  21.3 us
    pallas_call x1, Pallas kernels, attend_back(): call(run, (whole((rows, width), F32), whole((rows, width), BF), whole((8,...  10.9 us
    pallas_call x1, Pallas kernels, attend(): call(run, (whole((rows, half), BF), whole((keys, 2 * half), BF), whole((8...  10.7 us
  transfers between devices with their start and end apart: 83, of which 47 were waited for; matrix products, arithmetic and copies ran while one was open for 11% of the time, Pallas kernels for 22%

profile of v2, /device:TPU:0, one launch (start us, length us, event | category | flops | bytes accessed | tf_op | source)
XLA Modules:
  0.0 483.0 jit_solution(12229195567700266345)
XLA Ops:
  19.1 4.8 %collective-permute-done.1 = bf16[128,768]{1,0:T(8,128)(2,1)S(1)} collective-permute-done((bf16[128,768]{1,0:T(8,128)(2,1)S(1)}, bf16[128,768]{1,0:T(8,128)(2,1)S(1)}, u32[]{:S(2)}, u32[]{:S(2)}) %collective-permute-start.1) | collective-permute-done | bytes 196640 | tf_op jit(solution)/shard_map/ppermute | solution.py:27
  27.2 14.3 %all-gather.12.cloned.1.call-done = bf16[192,2816]{1,0:T(8,128)(2,1)} async-done(((bf16[48,2816]{1,0:T(8,128)(2,1)}), bf16[192,2816]{1,0:T(8,128)(2,1)}) %all-gather.12.cloned.1.call-update) | async-done | bytes 1081360 | tf_op jit(solution)/shard_map/all_gather | solution.py:261
  46.9 6.3 %collective-permute-done.4.refs_1_ = bf16[3,48,1280]{2,1,0:T(8,128)(2,1)S(1)} collective-permute-done((bf16[3,48,1280]{2,1,0:T(8,128)(2,1)S(1)}, bf16[3,48,1280]{2,1,0:T(8,128)(2,1)S(1)}, u32[]{:S(2)}, u32[]{:S(2)}) %collective-permute-start.4) | collective-permute-done | bytes 368672 | tf_op jit(solution)/shard_map/ppermute | solution.py:27
  66.7 9.5 %all-gather.14.cloned.1.call-done = bf16[192,3456]{1,0:T(8,128)(2,1)} async-done(((bf16[48,3456]{1,0:T(8,128)(2,1)}), bf16[192,3456]{1,0:T(8,128)(2,1)}) %all-gather.14.cloned.1.call-update) | async-done | bytes 1327120 | tf_op jit(solution)/shard_map/all_gather | solution.py:261
  82.0 4.5 assemble.2
  86.5 4.7 gru_open.1
  109.5 10.7 %attend.1 = (bf16[256,384]{1,0:T(8,128)(2,1)}, bf16[1024,768]{1,0:T(8,128)(2,1)}, f32[8,256]{1,0:T(8,128)}, bf16[256,384]{1,0:T(8,128)(2,1)}, f32[256,768]{1,0:T(8,128)}) custom-call(bf16[256,768]{1,0:T(8,128)(2,1)} %x_ref.3, bf16[3,256,768]{2,1,0:T(8,128)(2,1)} %pad_maximum_fusion.1.o_ref, bf16[768,1152]{1,0:T(8,128)(2,1)} %get-tuple-element.169.w_ref, ...), custom_call_target="tpu_custom_call" | custom-call | flops 1 | bytes 1 | tf_op jit(solution)/shard_map/attend/pallas_call | solution.py:701
  120.1 10.0 %collective-permute-done.15.refs_2_ = bf16[6,48,1664]{2,1,0:T(8,128)(2,1)S(1)} collective-permute-done((bf16[6,48,1664]{2,1,0:T(8,128)(2,1)}, bf16[6,48,1664]{2,1,0:T(8,128)(2,1)S(1)}, u32[]{:S(2)}, u32[]{:S(2)}) %collective-permute-start.15) | collective-permute-done | bytes 958496 | tf_op jit(solution)/shard_map/ppermute | solution.py:27
  131.1 5.3 %assemble.3 = (bf16[768,1536]{1,0:T(8,128)(2,1)}, bf16[768,384]{1,0:T(8,128)(2,1)}, bf16[768,1536]{1,0:T(8,128)(2,1)}) custom-call(bf16[3,48,1664]{2,1,0:T(8,128)(2,1)} %copy-done.4, bf16[3,48,1664]{2,1,0:T(8,128)(2,1)} %copy-done.10, bf16[6,48,1664]{2,1,0:T(8,128)(2,1)} %copy-done.19, bf16[3,48,1792]{2,1,0:T(8,128)(2,1)} %copy-done.3, ...), custom_call_target="tpu_custom_call" | custom-call | flops 1 | bytes 1 | tf_op jit(solution)/shard_map/assemble/pallas_call | solution.py:122
  137.3 6.7 %feed.1 = (f32[256,768]{1,0:T(8,128)}, f32[256,1]{1,0:T(8,128)}, bf16[256,768]{1,0:T(8,128)(2,1)}, f32[256,1536]{1,0:T(8,128)}, bf16[256,1536]{1,0:T(8,128)(2,1)}, /*index=5*/f32[256,768]{1,0:T(8,128)}) custom-call(bf16[256,768]{1,0:T(8,128)(2,1)} %x_ref.3, f32[256,768]{1,0:T(8,128)} %get-tuple-element.171.a_ref, f32[256,768]{1,0:T(8,128)} %copy-done.24, ...), custom_call_target="tpu_custom_call" | custom-call | flops 1 | bytes 1 | tf_op jit(solution)/shard_map/feed/pallas_call | solution.py:816
  166.9 5.2 %collective-permute-done.20.refs_1_ = bf16[272,384]{1,0:T(8,128)(2,1)S(1)} collective-permute-done((bf16[272,384]{1,0:T(8,128)(2,1)S(1)}, bf16[272,384]{1,0:T(8,128)(2,1)S(1)}, u32[]{:S(2)}, u32[]{:S(2)}) %collective-permute-start.20) | collective-permute-done | bytes 208928 | tf_op jit(solution)/shard_map/ppermute | solution.py:32
  172.2 6.8 %collective-permute-done.21.refs_2_ = bf16[272,384]{1,0:T(8,128)(2,1)S(1)} collective-permute-done((bf16[272,384]{1,0:T(8,128)(2,1)S(1)}, bf16[272,384]{1,0:T(8,128)(2,1)S(1)}, u32[]{:S(2)}, u32[]{:S(2)}) %collective-permute-start.21) | collective-permute-done | bytes 208928 | tf_op jit(solution)/shard_map/ppermute | solution.py:32
  179.7 6.7 %conv.1 = (f32[4,128,384]{2,1,0:T(8,128)}, f32[4,128,384]{2,1,0:T(8,128)}) custom-call(bf16[272,384]{1,0:T(8,128)(2,1)} %copy-done.11, bf16[272,384]{1,0:T(8,128)(2,1)} %copy-done.20, bf16[272,384]{1,0:T(8,128)(2,1)} %copy-done.21, bf16[272,384]{1,0:T(8,128)(2,1)} %copy-done.22, bf16[4,352,384]{2,1,0:T(8,128)(2,1)} %bitcast.98, bf16[3,768,384]{2,1,0:T(8,128)(2,1)} %bitcast.96), custom_call_target="tpu_custom_call" | custom-call | flops 1 | bytes 1 | tf_op jit(solution)/shard_map/conv/pallas_call | solution.py:329
  191.9 4.8 collective-permute-start.24
  200.2 6.9 %collective-permute-done.25.refs_2_ = bf16[128,384]{1,0:T(8,128)(2,1)S(1)} collective-permute-done((bf16[128,384]{1,0:T(8,128)(2,1)}, bf16[128,384]{1,0:T(8,128)(2,1)S(1)}, u32[]{:S(2)}, u32[]{:S(2)}) %collective-permute-start.25) | collective-permute-done | bytes 98336 | tf_op jit(solution)/shard_map/ppermute | solution.py:32
  212.2 5.6 %close.1 = (f32[256,768]{1,0:T(8,128)}, f32[384,768]{1,0:T(8,128)}, f32[256,768]{1,0:T(8,128)}, f32[384,768]{1,0:T(8,128)}, bf16[128,1536]{1,0:T(8,128)(2,1)}, /*index=5*/f32[8,768]{1,0:T(8,128)}) custom-call(f32[256,768]{1,0:T(8,128)} %get-tuple-element.181.s_ref, bf16[128,1536]{1,0:T(8,128)(2,1)} %side_by_side.1.ym_ref, bf16[128,1536]{1,0:T(8,128)(2,1)} %copy-done.42, ...), custom_call_target="tpu_custom_call" | custom-call | flops 1 | bytes 1 | tf_op jit(solution)/shard_map/close/pallas_call | solution.py:439
  238.2 6.0 %conv_grads.1 = bf16[4,3,192,384]{3,2,1,0:T(8,128)(2,1)} custom-call(bf16[272,384]{1,0:T(8,128)(2,1)} %copy-done.11, bf16[272,384]{1,0:T(8,128)(2,1)} %copy-done.20, bf16[272,384]{1,0:T(8,128)(2,1)} %copy-done.21, bf16[272,384]{1,0:T(8,128)(2,1)} %copy-done.22, bf16[4,352,384]{2,1,0:T(8,128)(2,1)} %bitcast.99, bf16[4,144,384]{2,1,0:T(8,128)(2,1)} %copy-done.5, ...), custom_call_target="tpu_custom_call" | custom-call | flops 1 | bytes 1 | tf_op jit(solution)/shard_map/conv_grads/pallas_call | solution.py:512
  244.5 5.9 %conv_back.1 = (bf16[256,384]{1,0:T(8,128)(2,1)}, bf16[256,384]{1,0:T(8,128)(2,1)}, bf16[256,384]{1,0:T(8,128)(2,1)}, bf16[256,384]{1,0:T(8,128)(2,1)}, bf16[256...) custom-call(bf16[4,144,384]{2,1,0:T(8,128)(2,1)} %copy-done.5, ...), custom_call_target="tpu_custom_call" | custom-call | flops 1 | bytes 1 | tf_op jit(solution)/shard_map/conv_back/pallas_call | solution.py:490
  253.8 4.7 collective-permute-done.37.refs_1_
  258.5 13.0 %collective-permute-done.38.refs_2_ = bf16[256,384]{1,0:T(8,128)(2,1)S(1)} collective-permute-done((bf16[256,384]{1,0:T(8,128)(2,1)}, bf16[256,384]{1,0:T(8,128)(2,1)S(1)}, u32[]{:S(2)}, u32[]{:S(2)}) %collective-permute-start.38) | collective-permute-done | bytes 196640 | tf_op jit(solution)/shard_map/ppermute | solution.py:32
  279.9 7.2 %feed_back.1 = (f32[256,768]{1,0:T(8,128)}, bf16[256,768]{1,0:T(8,128)(2,1)}, bf16[256,1536]{1,0:T(8,128)(2,1)}, f32[256,768]{1,0:T(8,128)}, f32[8,768]{1,0:T(8,128)}) custom-call(f32[256,768]{1,0:T(8,128)} %get-tuple-element.203.d_ref, f32[256,768]{1,0:T(8,128)} %get-tuple-element.211.a_ref, f32[256,768]{1,0:T(8,128)} %copy-done.25, ...), custom_call_target="tpu_custom_call" | custom-call | flops 1 | bytes 1 | tf_op jit(solution)/shard_map/feed_back/pallas_call | solution.py:888
  287.1 5.3 %collective-permute-done.35 = bf16[256,384]{1,0:T(8,128)(2,1)S(1)} collective-permute-done((bf16[256,384]{1,0:T(8,128)(2,1)}, bf16[256,384]{1,0:T(8,128)(2,1)S(1)}, u32[]{:S(2)}, u32[]{:S(2)}) %collective-permute-start.35) | collective-permute-done | bytes 196640 | tf_op jit(solution)/shard_map/ppermute | solution.py:32
  294.8 4.5 gru_back_open.1
  306.7 5.2 %gru_back_close.1 = (bf16[384,384]{1,0:T(8,128)(2,1)}, bf16[384,384]{1,0:T(8,128)(2,1)}, f32[8,768]{1,0:T(8,128)}, f32[384,768]{1,0:T(8,128)}) custom-call(f32[384,192]{1,0:T(8,128)} %get-tuple-element.220.cd, f32[384,192]{1,0:T(8,128)} %get-tuple-element.221.md, f32[384,192]{1,0:T(8,128)} %get-tuple-element.222.cu, f32[384,192]{1,0:T(8,128)} %get-tuple-element.223.mu, ...), custom_call_target="tpu_custom_call" | custom-call | flops 1 | bytes 1 | tf_op jit(solution)/shard_map/gru_back_close/pallas_call | solution.py:668
  311.9 4.6 grads.1
  324.1 10.9 %attend_back.1 = (f32[256,768]{1,0:T(8,128)}, bf16[256,768]{1,0:T(8,128)(2,1)}, f32[8,768]{1,0:T(8,128)}, bf16[256,384]{1,0:T(8,128)(2,1)}, f32[256,768]{1,0:T(8...) custom-call(f32[256,768]{1,0:T(8,128)} %get-tuple-element.236.d_ref, ...), custom_call_target="tpu_custom_call" | custom-call | flops 1 | bytes 1 | tf_op jit(solution)/shard_map/attend_back/pallas_call | solution.py:753
  355.6 4.3 collective-permute-start.46
  370.9 6.8 %query_grads.1 = (bf16[768,384]{1,0:T(8,128)(2,1)}, bf16[768,384]{1,0:T(8,128)(2,1)}, bf16[768,384]{1,0:T(8,128)(2,1)}, bf16[768,384]{1,0:T(8,128)(2,1)}, f32[256,768]{1,0:T(8,128)}) custom-call(bf16[256,768]{1,0:T(8,128)(2,1)} %x_ref.3, bf16[256,768]{1,0:T(8,128)(2,1)} %get-tuple-element.244.da_ref, bf16[256,384]{1,0:T(8,128)(2,1)} %get-tuple-element.245.att_ref, ...), custom_call_target="tpu_custom_call" | custom-call | flops 1 | bytes 1 | tf_op jit(solution)/shard_map/query_grads/pallas_call | solution.py:784
  385.2 9.1 %collective-permute-done.51.refs_1_ = bf16[768,384]{1,0:T(8,128)(2,1)} collective-permute-done((bf16[768,384]{1,0:T(8,128)(2,1)}, bf16[768,384]{1,0:T(8,128)(2,1)}, u32[]{:S(2)}, u32[]{:S(2)}) %collective-permute-start.51) | collective-permute-done | bytes 589856 | tf_op jit(solution)/shard_map/ppermute | solution.py:27
  399.8 7.9 %collective-permute-done.52.refs_2_ = bf16[768,384]{1,0:T(8,128)(2,1)} collective-permute-done((bf16[768,384]{1,0:T(8,128)(2,1)}, bf16[768,384]{1,0:T(8,128)(2,1)}, u32[]{:S(2)}, u32[]{:S(2)}) %collective-permute-start.52) | collective-permute-done | bytes 589856 | tf_op jit(solution)/shard_map/ppermute | solution.py:27
  410.6 4.8 collective-permute-done.55
  448.2 7.6 %collective-permute-done.74.refs_3_ = bf16[192,1152]{1,0:T(8,128)(2,1)S(1)} collective-permute-done((bf16[192,1152]{1,0:T(8,128)(2,1)S(1)}, bf16[192,1152]{1,0:T(8,128)(2,1)S(1)}, u32[]{:S(2)}, u32[]{:S(2)}) %collective-permute-start.74) | collective-permute-done | bytes 442400 | tf_op jit(solution)/shard_map/ppermute | solution.py:27
  (441 shorter events, 242.0 us)
Async XLA Ops:
  7.2 34.3 %all-gather.12.cloned.1.call-start = ((), (), s32[]{:S(2)}) async-start(), calls=%async_computation.6 | async-start | bytes 1351680 | tf_op jit(solution)/shard_map/all_gather | solution.py:261
  10.2 66.0 %all-gather.14.cloned.1.call-start = ((), (), s32[]{:S(2)}) async-start(), calls=%async_computation.7 | async-start | bytes 1658880 | tf_op jit(solution)/shard_map/all_gather | solution.py:261
  24.8 111.5 %all-gather.16.cloned.1.call-start = ((), (), s32[]{:S(2)}) async-start(), calls=%async_computation.8 | async-start | bytes 1351680 | tf_op jit(solution)/shard_map/all_gather | solution.py:261
  54.2 22.0 %collective-permute-start.5 = (bf16[6,48,1280]{2,1,0:T(8,128)(2,1)}, bf16[6,48,1280]{2,1,0:T(8,128)(2,1)S(1)}, u32[]{:S(2)}, u32[]{:S(2)}) collective-permute-start(bf16[6,48,1280]{2,1,0:T(8,128)(2,1)} %pad_maximum_fusion.9), channel_id=1, source_target_pairs={{0,4},{2,6},{4,0},{6,2},{1,5},{3,7},{5,1},{7,3},{8,12},{10,14},{12... | collective-permute-start | bytes 2211848 | tf_op jit(solution)/shard_map/ppermute | solution.py:27
  55.8 20.4 %collective-permute-start.7 = (bf16[6,48,1408]{2,1,0:T(8,128)(2,1)S(1)}, bf16[6,48,1408]{2,1,0:T(8,128)(2,1)S(1)}, u32[]{:S(2)}, u32[]{:S(2)}) collective-permute-start(bf16[6,48,1408]{2,1,0:T(8,128)(2,1)S(1)} %pad_maximum_fusion.7), channel_id=1, source_target_pairs={{0,2},{2,0},{4,6},{6,4},{1,3},{3,1},{5,7},{7,5},{8,10},{10,8},{12,... | collective-permute-start | bytes 2433032 | tf_op jit(solution)/shard_map/ppermute | solution.py:27
  104.9 139.6 %all-gather.18.cloned.1.call-start = ((), (), s32[]{:S(2)}) async-start(), calls=%async_computation.9 | async-start | bytes 4915200 | tf_op jit(solution)/shard_map/all_gather | solution.py:983
  105.3 25.0 %collective-permute-start.16 = (bf16[6,48,1792]{2,1,0:T(8,128)(2,1)S(1)}, bf16[6,48,1792]{2,1,0:T(8,128)(2,1)}, u32[]{:S(2)}, u32[]{:S(2)}) collective-permute-start(bf16[6,48,1792]{2,1,0:T(8,128)(2,1)S(1)} %pad_maximum_fusion.4), channel_id=1, source_target_pairs={{0,2},{2,0},{4,6},{6,4},{1,3},{3,1},{5,7},{7,5},{8,10},{10,8},{12,... | collective-permute-start | bytes 3096584 | tf_op jit(solution)/shard_map/ppermute | solution.py:27
  106.9 23.2 %collective-permute-start.15 = (bf16[6,48,1664]{2,1,0:T(8,128)(2,1)}, bf16[6,48,1664]{2,1,0:T(8,128)(2,1)S(1)}, u32[]{:S(2)}, u32[]{:S(2)}) collective-permute-start(bf16[6,48,1664]{2,1,0:T(8,128)(2,1)} %pad_maximum_fusion.6), channel_id=1, source_target_pairs={{0,4},{2,6},{4,0},{6,2},{1,5},{3,7},{5,1},{7,3},{8,12},{10,14},{12... | collective-permute-start | bytes 2875400 | tf_op jit(solution)/shard_map/ppermute | solution.py:27
  147.2 230.5 %reduce-scatter.10.cloned.1.call-start = ((), (), s32[]{:S(2)}) async-start(), calls=%async_computation.10 | async-start | bytes 2211840
  244.3 138.3 %reduce-scatter.6.cloned.1.call-start = ((), (), s32[]{:S(2)}) async-start(), calls=%async_computation.3 | async-start | bytes 2949120 | tf_op jit(solution)/shard_map/reduce_scatter | solution.py:1030
  252.9 18.7 %collective-permute-start.38 = (bf16[256,384]{1,0:T(8,128)(2,1)}, bf16[256,384]{1,0:T(8,128)(2,1)S(1)}, u32[]{:S(2)}, u32[]{:S(2)}) collective-permute-start(bf16[256,384]{1,0:T(8,128)(2,1)} %get-tuple-element.206), channel_id=1, source_target_pairs={{0,16},{8,24},{16,0},{24,8},{1,17},{9,25},{17,1},{25,9},{2,18},{10... | collective-permute-start | bytes 589832 | tf_op jit(solution)/shard_map/ppermute | solution.py:32
  253.8 17.8 %collective-permute-start.39 = (bf16[256,384]{1,0:T(8,128)(2,1)}, bf16[256,384]{1,0:T(8,128)(2,1)S(1)}, u32[]{:S(2)}, u32[]{:S(2)}) collective-permute-start(bf16[256,384]{1,0:T(8,128)(2,1)} %get-tuple-element.207), channel_id=1, source_target_pairs={{0,8},{8,16},{16,24},{24,0},{1,9},{9,17},{17,25},{25,1},{2,10},{10... | collective-permute-start | bytes 589832 | tf_op jit(solution)/shard_map/ppermute | solution.py:32
  275.0 17.4 %collective-permute-start.35 = (bf16[256,384]{1,0:T(8,128)(2,1)}, bf16[256,384]{1,0:T(8,128)(2,1)S(1)}, u32[]{:S(2)}, u32[]{:S(2)}) collective-permute-start(bf16[256,384]{1,0:T(8,128)(2,1)} %get-tuple-element.200), channel_id=1, source_target_pairs={{0,16},{8,24},{16,0},{24,8},{1,17},{9,25},{17,1},{25,9},{2,18},{10... | collective-permute-start | bytes 589832 | tf_op jit(solution)/shard_map/ppermute | solution.py:32
  316.5 104.2 %reduce-scatter.8.cloned.1.call-start = ((), (), s32[]{:S(2)}) async-start(), calls=%async_computation.4 | async-start | bytes 1474560 | tf_op jit(solution)/shard_map/reduce_scatter | solution.py:1040
  319.4 17.8 %collective-permute-start.69 = (bf16[512,384]{1,0:T(8,128)(2,1)S(1)}, bf16[512,384]{1,0:T(8,128)(2,1)S(1)}, u32[]{:S(2)}, u32[]{:S(2)}) collective-permute-start(bf16[512,384]{1,0:T(8,128)(2,1)S(1)} %get-tuple-element.380), channel_id=1, source_target_pairs={{0,4},{2,6},{4,0},{6,2},{1,5},{3,7},{5,1},{7,3},{8,12},{10,14},{12... | collective-permute-start | bytes 1179656 | tf_op jit(solution)/shard_map/ppermute | solution.py:27
  320.2 18.6 %collective-permute-start.70 = (bf16[512,384]{1,0:T(8,128)(2,1)S(1)}, bf16[512,384]{1,0:T(8,128)(2,1)S(1)}, u32[]{:S(2)}, u32[]{:S(2)}) collective-permute-start(bf16[512,384]{1,0:T(8,128)(2,1)S(1)} %get-tuple-element.379), channel_id=1, source_target_pairs={{0,6},{2,4},{4,2},{6,0},{1,7},{3,5},{5,3},{7,1},{8,14},{10,12},{12... | collective-permute-start | bytes 1179656 | tf_op jit(solution)/shard_map/ppermute | solution.py:27
  343.8 116.8 %all-gather.10.cloned.1.call-start = ((), (), s32[]{:S(2)}) async-start(), calls=%async_computation.5 | async-start | bytes 2211840 | tf_op jit(solution)/shard_map/all_gather | solution.py:1031
  344.3 37.0 %collective-permute-start.60 = (f32[384,768]{1,0:T(8,128)S(1)}, f32[384,768]{1,0:T(8,128)S(1)}, u32[]{:S(2)}, u32[]{:S(2)}) collective-permute-start(f32[384,768]{1,0:T(8,128)S(1)} %copy-done.18), channel_id=1, source_target_pairs={{0,1},{1,0},{2,3},{3,2},{4,5},{5,4},{6,7},{7,6},{8,9},{9,8},{10,11... | collective-permute-start | bytes 3538952 | tf_op jit(solution)/shard_map/ppermute | solution.py:27
  344.8 25.1 %collective-permute-start.48 = (bf16[256,768]{1,0:T(8,128)(2,1)}, bf16[256,768]{1,0:T(8,128)(2,1)S(1)}, u32[]{:S(2)}, u32[]{:S(2)}) collective-permute-start(bf16[256,768]{1,0:T(8,128)(2,1)} %get-tuple-element.248), channel_id=1, source_target_pairs={{0,2},{2,0},{4,6},{6,4},{1,3},{3,1},{5,7},{7,5},{8,10},{10,8},{12,... | collective-permute-start | bytes 1179656 | tf_op jit(solution)/shard_map/ppermute | solution.py:27
  345.6 24.3 %collective-permute-start.49 = (bf16[256,768]{1,0:T(8,128)(2,1)}, bf16[256,768]{1,0:T(8,128)(2,1)S(1)}, u32[]{:S(2)}, u32[]{:S(2)}) collective-permute-start(bf16[256,768]{1,0:T(8,128)(2,1)} %get-tuple-element.249), channel_id=1, source_target_pairs={{0,4},{2,6},{4,0},{6,2},{1,5},{3,7},{5,1},{7,3},{8,12},{10,14},{12... | collective-permute-start | bytes 1179656 | tf_op jit(solution)/shard_map/ppermute | solution.py:27
  347.1 22.9 %collective-permute-start.50 = (bf16[256,768]{1,0:T(8,128)(2,1)}, bf16[256,768]{1,0:T(8,128)(2,1)S(1)}, u32[]{:S(2)}, u32[]{:S(2)}) collective-permute-start(bf16[256,768]{1,0:T(8,128)(2,1)} %get-tuple-element.250), channel_id=1, source_target_pairs={{0,6},{2,4},{4,2},{6,0},{1,7},{3,5},{5,3},{7,1},{8,14},{10,12},{12... | collective-permute-start | bytes 1179656 | tf_op jit(solution)/shard_map/ppermute | solution.py:27
  377.7 18.0 %collective-permute-start.59 = (f32[256,768]{1,0:T(8,128)}, f32[256,768]{1,0:T(8,128)}, u32[]{:S(2)}, u32[]{:S(2)}) collective-permute-start(f32[256,768]{1,0:T(8,128)} %get-tuple-element.263), channel_id=1, source_target_pairs={{0,1},{1,0},{2,3},{3,2},{4,5},{5,4},{6,7},{7,6},{8,9},{9,8},{10,11... | collective-permute-start | bytes 2359304 | tf_op jit(solution)/shard_map/ppermute | solution.py:27
  379.3 28.4 %collective-permute-start.52 = (bf16[768,384]{1,0:T(8,128)(2,1)}, bf16[768,384]{1,0:T(8,128)(2,1)}, u32[]{:S(2)}, u32[]{:S(2)}) collective-permute-start(bf16[768,384]{1,0:T(8,128)(2,1)} %get-tuple-element.255), channel_id=1, source_target_pairs={{0,4},{2,6},{4,0},{6,2},{1,5},{3,7},{5,1},{7,3},{8,12},{10,14},{12... | collective-permute-start | bytes 1769480 | tf_op jit(solution)/shard_map/ppermute | solution.py:27
  380.8 27.1 %collective-permute-start.53 = (bf16[768,384]{1,0:T(8,128)(2,1)}, bf16[768,384]{1,0:T(8,128)(2,1)}, u32[]{:S(2)}, u32[]{:S(2)}) collective-permute-start(bf16[768,384]{1,0:T(8,128)(2,1)} %get-tuple-element.256), channel_id=1, source_target_pairs={{0,6},{2,4},{4,2},{6,0},{1,7},{3,5},{5,3},{7,1},{8,14},{10,12},{12... | collective-permute-start | bytes 1769480 | tf_op jit(solution)/shard_map/ppermute | solution.py:27
  383.6 26.9 %collective-permute-start.54 = (bf16[192,384]{1,0:T(8,128)(2,1)S(1)}, bf16[192,384]{1,0:T(8,128)(2,1)S(1)}, u32[]{:S(2)}, u32[]{:S(2)}) collective-permute-start(bf16[192,384]{1,0:T(8,128)(2,1)S(1)} %get-tuple-element.364), channel_id=1, source_target_pairs={{0,2},{2,0},{4,6},{6,4},{1,3},{3,1},{5,7},{7,5},{8,10},{10,8},{12,... | collective-permute-start | bytes 442376 | tf_op jit(solution)/shard_map/ppermute | solution.py:27
  394.3 21.1 %collective-permute-start.55 = (bf16[192,384]{1,0:T(8,128)(2,1)S(1)}, bf16[192,384]{1,0:T(8,128)(2,1)S(1)}, u32[]{:S(2)}, u32[]{:S(2)}) collective-permute-start(bf16[192,384]{1,0:T(8,128)(2,1)S(1)} %get-tuple-element.363), channel_id=1, source_target_pairs={{0,4},{2,6},{4,0},{6,2},{1,5},{3,7},{5,1},{7,3},{8,12},{10,14},{12... | collective-permute-start | bytes 442376 | tf_op jit(solution)/shard_map/ppermute | solution.py:27
  395.7 21.5 %collective-permute-start.56 = (bf16[192,384]{1,0:T(8,128)(2,1)S(1)}, bf16[192,384]{1,0:T(8,128)(2,1)S(1)}, u32[]{:S(2)}, u32[]{:S(2)}) collective-permute-start(bf16[192,384]{1,0:T(8,128)(2,1)S(1)} %get-tuple-element.362), channel_id=1, source_target_pairs={{0,6},{2,4},{4,2},{6,0},{1,7},{3,5},{5,3},{7,1},{8,14},{10,12},{12... | collective-permute-start | bytes 442376 | tf_op jit(solution)/shard_map/ppermute | solution.py:27
  426.4 21.2 %collective-permute-start.72 = (bf16[192,1152]{1,0:T(8,128)(2,1)S(1)}, bf16[192,1152]{1,0:T(8,128)(2,1)S(1)}, u32[]{:S(2)}, u32[]{:S(2)}) collective-permute-start(bf16[192,1152]{1,0:T(8,128)(2,1)S(1)} %pad_maximum_fusion.19.refs_0_), channel_id=1, source_target_pairs={{0,2},{2,0},{4,6},{6,4},{1,3},{3,1},{5,7},{7,5},{8,10},{10,8},{12,... | collective-permute-start | bytes 1327112 | tf_op jit(solution)/shard_map/ppermute | solution.py:27
  428.4 19.8 %collective-permute-start.73 = (bf16[192,1152]{1,0:T(8,128)(2,1)S(1)}, bf16[192,1152]{1,0:T(8,128)(2,1)S(1)}, u32[]{:S(2)}, u32[]{:S(2)}) collective-permute-start(bf16[192,1152]{1,0:T(8,128)(2,1)S(1)} %pad_maximum_fusion.19.refs_0_), channel_id=1, source_target_pairs={{0,4},{2,6},{4,0},{6,2},{1,5},{3,7},{5,1},{7,3},{8,12},{10,14},{12... | collective-permute-start | bytes 1327112 | tf_op jit(solution)/shard_map/ppermute | solution.py:27
  429.6 26.2 %collective-permute-start.74 = (bf16[192,1152]{1,0:T(8,128)(2,1)S(1)}, bf16[192,1152]{1,0:T(8,128)(2,1)S(1)}, u32[]{:S(2)}, u32[]{:S(2)}) collective-permute-start(bf16[192,1152]{1,0:T(8,128)(2,1)S(1)} %pad_maximum_fusion.19.refs_0_), channel_id=1, source_target_pairs={{0,6},{2,4},{4,2},{6,0},{1,7},{3,5},{5,3},{7,1},{8,14},{10,12},{12... | collective-permute-start | bytes 1327112 | tf_op jit(solution)/shard_map/ppermute | solution.py:27
  444.6 19.8 %collective-permute-start.64 = (bf16[192,384]{1,0:T(8,128)(2,1)S(1)}, bf16[192,384]{1,0:T(8,128)(2,1)S(1)}, u32[]{:S(2)}, u32[]{:S(2)}) collective-permute-start(bf16[192,384]{1,0:T(8,128)(2,1)S(1)} %add_convert_fusion.3.refs_0_), channel_id=1, source_target_pairs={{0,2},{2,0},{4,6},{6,4},{1,3},{3,1},{5,7},{7,5},{8,10},{10,8},{12,... | collective-permute-start | bytes 442376 | tf_op jit(solution)/shard_map/ppermute | solution.py:27
  446.2 18.3 %collective-permute-start.65 = (bf16[192,384]{1,0:T(8,128)(2,1)S(1)}, bf16[192,384]{1,0:T(8,128)(2,1)S(1)}, u32[]{:S(2)}, u32[]{:S(2)}) collective-permute-start(bf16[192,384]{1,0:T(8,128)(2,1)S(1)} %add_convert_fusion.3.refs_0_), channel_id=1, source_target_pairs={{0,4},{2,6},{4,0},{6,2},{1,5},{3,7},{5,1},{7,3},{8,12},{10,14},{12... | collective-permute-start | bytes 442376 | tf_op jit(solution)/shard_map/ppermute | solution.py:27
  (127 other events, 880.3 us)
Sparse Core Ops, SparseCore 0:
  10.3 31.1 all-gather.11
  43.7 32.4 all-gather.13
  105.0 26.5 all-gather.15
  147.3 49.5 all-gather.17
  244.4 31.6 reduce-scatter.9
  316.6 50.4 reduce-scatter.5
  370.0 28.6 reduce-scatter.7
  400.5 41.8 all-gather.9
